TPU v7x, 32 devices: a whole 2x2x4 slice. The times are simulated.
32 devices in a mesh: gx: 4 (over z), gy: 4 (over x, core), gz: 2 (over y).
Axes of the slice: x: 2, y: 2, z: 4, core: 2. Of those that a mesh axis runs over, the one named last changes fastest.
Arguments:
- vel: float32 [3, 64, 64, 512], P(None, 'gz', 'gx', 'gy'), may hold values from -6 to 6
- pres: float32 [64, 64, 512], P('gz', 'gx', 'gy'), may hold values from -6 to 6
- modulus: float32 [64, 64, 512], P('gz', 'gx', 'gy'), may hold values from 0.05 to 0.5
- adj_vel_in: float32 [3, 64, 64, 512], P(None, 'gz', 'gx', 'gy'), may hold values from -6 to 6
- adj_pres_in: float32 [64, 64, 512], P('gz', 'gx', 'gy'), may hold values from -6 to 6
- sensor_values: float32 [1024, 128], P(('gx', 'gy', 'gz')), may hold values from -6 to 6
- sensor_owner: int32 [1024, 1], P(('gx', 'gy', 'gz')), may hold values from 0 to 15; in each aligned block of 32 rows (0 to 31, 32 to 63, ...) at most 4 rows name the same one
- sensor_line: int32 [1024], P(('gx', 'gy', 'gz')), may hold values from 0 to 15
- sensor_step: int32 [1024], P(('gx', 'gy', 'gz')), may hold values from 0 to 1
Outputs:
- adj_vel: float32 [3, 64, 64, 512], P(None, 'gz', 'gx', 'gy')
- adj_pres: float32 [64, 64, 512], P('gz', 'gx', 'gy')
- shear_gradient: float32 [64, 64, 512], P('gz', 'gx', 'gy')
Inputs may be any that keep to these rules, and one draw needn't show every extreme that they name: `sensor_owner`: among the 32 rows of one device at most 4 name the same surface brick, and in every draw some device has 4 rows for one brick.
All inputs are finite; a program needn't handle non-finite values.
Results may differ from a plain program's by a relative error of at most 0.00011.
Values sent between devices are 32-bit elements; how exact they have to be, the bound alone decides.
No kernel may reach another device: no remote copies, remote signals or barrier semaphores. Data moves between devices by JAX's collectives and lax.ppermute only.
A program may use at most 64 MiB of HBM per device.

v0:
```python
import jax
import jax.numpy as jnp
from jax import lax
from jax.sharding import PartitionSpec as P

STEPS = 2


def shifted(value, axis, by):
    peers = lax.axis_size(axis)
    pairs = [(i, i + by) for i in range(peers) if 0 <= i + by < peers]
    return lax.ppermute(value, axis, pairs)


def extended(block, sides, width):
    for axis, dim in sides:
        count = lax.axis_size(axis)
        forward = [(i, i + 1) for i in range(count - 1)]
        backward = [(target, source) for source, target in forward]
        low = lax.ppermute(
            lax.slice_in_dim(block, block.shape[dim] - width, None, axis=dim), axis, forward
        )
        high = lax.ppermute(lax.slice_in_dim(block, 0, width, axis=dim), axis, backward)
        block = jnp.concatenate([low, block, high], axis=dim)
    return block


def inner(padded):
    return padded[:, 1:-1, 1:-1, 1:-1]


def laplace(padded):
    center = inner(padded)
    total = padded[:, 2:, 1:-1, 1:-1] + padded[:, :-2, 1:-1, 1:-1]
    total = total + padded[:, 1:-1, 2:, 1:-1] + padded[:, 1:-1, :-2, 1:-1]
    total = total + padded[:, 1:-1, 1:-1, 2:] + padded[:, 1:-1, 1:-1, :-2]
    return total - 6.0 * center


def divergence(padded):
    center = inner(padded)
    along_x = center[0] - padded[0, 1:-1, :-2, 1:-1]
    along_y = center[1] - padded[1, 1:-1, 1:-1, :-2]
    along_z = center[2] - padded[2, :-2, 1:-1, 1:-1]
    return along_x + along_y + along_z


def gradient(field):
    next_x = shifted(field[:, 0:1, :], "gx", -1)
    next_y = shifted(field[:, :, 0:1], "gy", -1)
    next_z = shifted(field[0:1], "gz", -1)
    upper_x = jnp.concatenate([field[:, 1:, :], next_x], axis=1)
    upper_y = jnp.concatenate([field[:, :, 1:], next_y], axis=2)
    upper_z = jnp.concatenate([field[1:], next_z], axis=0)
    return jnp.stack([upper_x - field, upper_y - field, upper_z - field])


def adjoint_halo(stacked):
    return extended(stacked, (("gx", 2), ("gy", 3), ("gz", 1)), 1)


def shards(
    vel,
    pres,
    modulus,
    adj_vel_in,
    adj_pres_in,
    sensor_values,
    sensor_owner,
    sensor_line,
    sensor_step,
):
    owners = lax.axis_size("gx") * lax.axis_size("gy")
    rows = sensor_values.shape[0]
    lines = vel.shape[2]
    code = sensor_step * lines + sensor_line
    owner = sensor_owner[:, 0]
    target = owner * (STEPS * lines) + code
    table = (
        lax.broadcasted_iota(jnp.int32, (owners * STEPS * lines, rows), 0) == target[None, :]
    ).astype(jnp.float32)
    spread = jnp.dot(
        table, sensor_values, precision=lax.Precision.HIGHEST, preferred_element_type=jnp.float32
    )
    forcing = lax.psum_scatter(spread, ("gx", "gy"), scatter_dimension=0, tiled=True)
    forcing = lax.psum(forcing, "gz")
    surface = (lax.axis_index("gz") == 0).astype(jnp.float32)
    forcing = surface * forcing.reshape(STEPS, lines, forcing.shape[1])
    saved = []
    state_v, state_p = (vel, pres)
    for step in range(STEPS):
        padded = extended(state_v, (("gx", 2), ("gy", 3), ("gz", 1)), 1)
        bend = laplace(padded)
        saved.append(bend)
        if step + 1 < STEPS:
            state_p = state_p + 1.0 * divergence(padded)
            state_v = state_v + 0.25 * (gradient(state_p) + modulus[None] * bend)
    lam_v, lam_p = (adj_vel_in, adj_pres_in)
    shear = jnp.zeros(pres.shape, jnp.float32)
    for step in reversed(range(STEPS)):
        lam_v = lam_v.at[2, 0].add(forcing[step])
        both = adjoint_halo(jnp.concatenate([lam_v, modulus[None] * lam_v], axis=0))
        padded = both[:3]
        weighted = laplace(both[3:])
        shear = shear + 0.25 * jnp.sum(lam_v * saved[step], axis=0)
        middle = lam_p - 0.25 * divergence(padded)
        lam_v = lam_v + 0.25 * weighted - 1.0 * gradient(middle)
        lam_p = middle
    return (lam_v, lam_p, shear)


def solution(mesh):
    return jax.shard_map(
        shards,
        mesh=mesh,
        in_specs=(
            P(None, "gz", "gx", "gy"),
            P("gz", "gx", "gy"),
            P("gz", "gx", "gy"),
            P(None, "gz", "gx", "gy"),
            P("gz", "gx", "gy"),
            P(("gx", "gy", "gz"), None),
            P(("gx", "gy", "gz"), None),
            P(("gx", "gy", "gz")),
            P(("gx", "gy", "gz")),
        ),
        out_specs=(P(None, "gz", "gx", "gy"), P("gz", "gx", "gy"), P("gz", "gx", "gy")),
        check_vma=False,
    )
```

profile of v0, /device:TPU:0, one launch (start us, length us, event | category | flops | bytes accessed | tf_op | source)
XLA Modules:
  0.0 242.4 jit_solution(11530727187835036880)
XLA Ops:
  10.2 4.9 %collective-permute-start.18 = (f32[3,32,1,128]{3,2,1,0:T(1,128)S(1)}, f32[3,32,1,128]{3,2,1,0:T(1,128)S(1)}, u32[]{:S(2)}, u32[]{:S(2)}) collective-permute-start(f32[3,32,1,128]{3,2,1,0:T(1,128)S(1)} %get-tuple-element.51), channel_id=1, source_target_pairs={{0,8},{8,16},{16,24},{1,9},{9,17},{17,25},{2,10},{10,18},{18,26},{... | collective-permute-start | bytes 147464 | tf_op jit(solution)/shard_map/ppermute | solution.py:20
  16.9 4.2 %collective-permute-done.19 = f32[3,32,1,128]{3,2,1,0:T(1,128)S(1)} collective-permute-done((f32[3,32,1,128]{3,2,1,0:T(1,128)S(1)}, f32[3,32,1,128]{3,2,1,0:T(1,128)S(1)}, u32[]{:S(2)}, u32[]{:S(2)}) %collective-permute-start.19) | collective-permute-done | bytes 49184 | tf_op jit(solution)/shard_map/ppermute | solution.py:23
  22.4 47.8 %reduce-scatter.2.cloned.1.call-done = f32[32,128]{1,0:T(8,128)} async-done(((f32[512,128]{1,0:T(8,128)}), f32[32,128]{1,0:T(8,128)}) %reduce-scatter.2.cloned.1.call-update) | async-done | bytes 16400 | tf_op jit(solution)/shard_map/reduce_scatter | solution.py:85
  70.2 8.8 %psum.7 = f32[32,128]{1,0:T(8,128)S(1)} all-reduce(f32[32,128]{1,0:T(8,128)} %reduce-scatter.2.cloned.1.call-done), channel_id=1, replica_groups=mesh['gx'=4,'gy'=4,'gz'=2] {'gz'}, use_global_device_ids=true, to_apply=%region_1.0 | all-reduce | flops 4096 | bytes 32768 | tf_op jit(solution)/shard_map/psum | solution.py:86
  79.2 3.4 %collective-permute-start = (f32[6,32,1,128]{3,2,1,0:T(1,128)S(1)}, f32[6,32,1,128]{3,2,1,0:T(1,128)S(1)}, u32[]{:S(2)}, u32[]{:S(2)}) collective-permute-start(f32[6,32,1,128]{3,2,1,0:T(1,128)S(1)} %get-tuple-element.43), channel_id=1, source_target_pairs={{0,8},{8,16},{16,24},{1,9},{9,17},{17,25},{2,10},{10,18},{18,26},{... | collective-permute-start | bytes 294920 | tf_op jit(solution)/shard_map/ppermute | solution.py:20
  93.1 2.0 collective-permute-done.21
  97.0 2.9 %fusion.65 = (f32[6,32,18,1]{3,2,1,0:T(8,128)}, f32[6,32,18,1]{3,2,1,0:T(8,128)}) fusion(f32[6,32,18,128]{3,2,1,0:T(8,128)S(1)} %pad_maximum_fusion), kind=kLoop, calls=%fused_computation.206 | loop fusion | bytes 55296 | tf_op jit(solution)/shard_map/slice | solution.py:23
  99.9 2.4 copy.12
  102.3 4.5 %collective-permute-start.2 = (f32[6,32,18,1]{1,3,2,0:T(1,128)S(1)}, f32[6,32,18,1]{1,3,2,0:T(1,128)S(1)}, u32[]{:S(2)}, u32[]{:S(2)}) collective-permute-start(f32[6,32,18,1]{1,3,2,0:T(1,128)S(1)} %copy.12), channel_id=1, source_target_pairs={{0,2},{2,4},{4,6},{1,3},{3,5},{5,7},{8,10},{10,12},{12,14},{9,11},... | collective-permute-start | bytes 41480 | tf_op jit(solution)/shard_map/ppermute | solution.py:20
  106.7 2.4 copy.13
  112.0 2.5 %collective-permute-start.22 = (f32[3,1,18,130]{3,2,1,0:T(8,128)S(1)}, f32[3,1,18,130]{3,2,1,0:T(8,128)S(1)}, u32[]{:S(2)}, u32[]{:S(2)}) collective-permute-start(f32[3,1,18,130]{3,2,1,0:T(8,128)S(1)} %get-tuple-element.36), channel_id=1, source_target_pairs={{0,1},{2,3},{4,5},{6,7},{8,9},{10,11},{12,13},{14,15},{16,17},{18,... | collective-permute-start | bytes 84248 | tf_op jit(solution)/shard_map/ppermute | solution.py:20
  115.8 2.3 copy.14
  118.1 2.3 copy.15
  121.8 5.4 %collective-permute-start.5 = (f32[6,1,18,130]{3,2,1,0:T(8,128)S(1)}, f32[6,1,18,130]{3,2,1,0:T(8,128)S(1)}, u32[]{:S(2)}, u32[]{:S(2)}) collective-permute-start(f32[6,1,18,130]{3,2,1,0:T(8,128)S(1)} %get-tuple-element.32), channel_id=1, source_target_pairs={{0,1},{2,3},{4,5},{6,7},{8,9},{10,11},{12,13},{14,15},{16,17},{18,... | collective-permute-start | bytes 168488 | tf_op jit(solution)/shard_map/ppermute | solution.py:20
  139.3 2.4 %collective-permute-done.8 = f32[1,16,128]{2,1,0:T(8,128)S(1)} collective-permute-done((f32[1,16,128]{2,1,0:T(8,128)S(1)}, f32[1,16,128]{2,1,0:T(8,128)S(1)}, u32[]{:S(2)}, u32[]{:S(2)}) %collective-permute-start.8) | collective-permute-done | bytes 8224 | tf_op jit(solution)/shard_map/ppermute | solution.py:12
  141.9 4.1 %collective-permute-done.4 = f32[6,1,18,130]{3,2,1,0:T(8,128)S(1)} collective-permute-done((f32[6,1,18,130]{3,2,1,0:T(8,128)S(1)}, f32[6,1,18,130]{3,2,1,0:T(8,128)S(1)}, u32[]{:S(2)}, u32[]{:S(2)}) %collective-permute-start.4) | collective-permute-done | bytes 56192 | tf_op jit(solution)/shard_map/ppermute | solution.py:23
  146.0 2.7 %fusion.23 = f32[3,32,16,128]{3,2,1,0:T(8,128)S(1)} fusion(f32[3,32,16,128]{3,2,1,0:T(8,128)S(1)} %fusion.62, f32[6,32,18,1]{3,2,1,0:T(8,128)S(1)} %copy-done.2, f32[6,32,1,128]{3,2,1,0:T(1,128)S(1)} %copy-done.16, f32[6,32,1,128]{3,2,1,0:T(1,128)S(1)} %collective-permute-done, f32[3,32,16,128]{3,2,1,0:T(8,128)S(1)} %broadcast_multiply_fusion.1, ...), kind=kLoop, calls=%fused_computation.79 | loop fusion | flops 7077888 | bytes 3482304 | tf_op jit(solution)/shard_map/sub | solution.py:107
  148.8 4.0 %multiply_reduce_fusion = (f32[32,16,128]{2,1,0:T(8,128)}, f32[3,32,16,128]{3,2,1,0:T(8,128)S(1)}) fusion(f32[3,32,16,128]{3,2,1,0:T(8,128)S(1)} %fusion.60, f32[3,32,16,128]{3,2,1,0:T(8,128)S(1)} %copy-done.6, f32[3,32,1,128]{3,2,1,0:T(1,128)S(1)} %copy-done.25, f32[3,32,1,128]{3,2,1,0:T(1,128)S(1)} %copy-done.23, f32[3,32,18,1]{3,2,1,0:T(8,128)S(1)} %copy-done.7, ...), kind=kLoop, calls=%fused_computation.99 | loop fusion | flops 5242880 | bytes 2789728 | tf_op jit(solution)/shard_map/reduce_sum | solution.py:105
  153.2 5.2 %collective-permute-start.27 = (f32[3,32,1,128]{3,2,1,0:T(1,128)S(1)}, f32[3,32,1,128]{3,2,1,0:T(1,128)S(1)}, u32[]{:S(2)}, u32[]{:S(2)}) collective-permute-start(f32[3,32,1,128]{3,2,1,0:T(1,128)S(1)} %get-tuple-element.49), channel_id=1, source_target_pairs={{0,8},{8,16},{16,24},{1,9},{9,17},{17,25},{2,10},{10,18},{18,26},{... | collective-permute-start | bytes 147464 | tf_op jit(solution)/shard_map/ppermute | solution.py:20
  161.3 5.4 %collective-permute-start.9 = (f32[6,32,1,128]{3,2,1,0:T(1,128)S(1)}, f32[6,32,1,128]{3,2,1,0:T(1,128)S(1)}, u32[]{:S(2)}, u32[]{:S(2)}) collective-permute-start(f32[6,32,1,128]{3,2,1,0:T(1,128)S(1)} %get-tuple-element.41), channel_id=1, source_target_pairs={{0,8},{8,16},{16,24},{1,9},{9,17},{17,25},{2,10},{10,18},{18,26},{... | collective-permute-start | bytes 294920 | tf_op jit(solution)/shard_map/ppermute | solution.py:20
  176.3 3.3 %collective-permute-done.30 = f32[3,32,18,1]{1,3,2,0:T(1,128)S(1)} collective-permute-done((f32[3,32,18,1]{1,3,2,0:T(1,128)S(1)}, f32[3,32,18,1]{1,3,2,0:T(1,128)S(1)}, u32[]{:S(2)}, u32[]{:S(2)}) %collective-permute-start.30) | collective-permute-done | bytes 6944 | tf_op jit(solution)/shard_map/ppermute | solution.py:23
  181.5 2.9 %fusion.64 = (f32[6,32,18,1]{3,2,1,0:T(8,128)}, f32[6,32,18,1]{3,2,1,0:T(8,128)}) fusion(f32[6,32,18,128]{3,2,1,0:T(8,128)S(1)} %pad_maximum_fusion.1), kind=kLoop, calls=%fused_computation.205 | loop fusion | bytes 55296 | tf_op jit(solution)/shard_map/slice | solution.py:23
  184.4 3.1 %copy.18 = f32[6,32,18,1]{1,3,2,0:T(1,128)} copy(f32[6,32,18,1]{3,2,1,0:T(8,128)} %get-tuple-element.38) | data formatting | bytes 27648 | tf_op jit(solution)/shard_map/slice | solution.py:21
  187.5 5.1 %collective-permute-start.11 = (f32[6,32,18,1]{1,3,2,0:T(1,128)}, f32[6,32,18,1]{1,3,2,0:T(1,128)}, u32[]{:S(2)}, u32[]{:S(2)}) collective-permute-start(f32[6,32,18,1]{1,3,2,0:T(1,128)} %copy.18), channel_id=1, source_target_pairs={{0,2},{2,4},{4,6},{1,3},{3,5},{5,7},{8,10},{10,12},{12,14},{9,11},... | collective-permute-start | bytes 41480 | tf_op jit(solution)/shard_map/ppermute | solution.py:20
  192.6 3.0 %copy.19 = f32[6,32,18,1]{1,3,2,0:T(1,128)} copy(f32[6,32,18,1]{3,2,1,0:T(8,128)} %get-tuple-element.37) | data formatting | bytes 27648 | tf_op jit(solution)/shard_map/slice | solution.py:23
  199.8 5.8 %collective-permute-start.32 = (f32[3,1,18,130]{3,2,1,0:T(8,128)}, f32[3,1,18,130]{3,2,1,0:T(8,128)}, u32[]{:S(2)}, u32[]{:S(2)}) collective-permute-start(f32[3,1,18,130]{3,2,1,0:T(8,128)} %get-tuple-element.34), channel_id=1, source_target_pairs={{0,1},{2,3},{4,5},{6,7},{8,9},{10,11},{12,13},{14,15},{16,17},{18,... | collective-permute-start | bytes 84248 | tf_op jit(solution)/shard_map/ppermute | solution.py:20
  205.6 3.1 %copy.20 = f32[6,32,18,1]{3,2,1,0:T(8,128)} copy(f32[6,32,18,1]{1,3,2,0:T(1,128)} %collective-permute-done.11) | data formatting | bytes 27648 | tf_op jit(solution)/shard_map/ppermute | solution.py:20
  208.7 3.1 %copy.21 = f32[6,32,18,1]{3,2,1,0:T(8,128)} copy(f32[6,32,18,1]{1,3,2,0:T(1,128)} %collective-permute-done.12) | data formatting | bytes 27648 | tf_op jit(solution)/shard_map/ppermute | solution.py:23
  214.8 2.2 fusion.3
  225.3 2.0 collective-permute-done.17
  227.5 4.7 %collective-permute-done.13 = f32[6,1,18,130]{3,2,1,0:T(8,128)S(1)} collective-permute-done((f32[6,1,18,130]{3,2,1,0:T(8,128)S(1)}, f32[6,1,18,130]{3,2,1,0:T(8,128)S(1)}, u32[]{:S(2)}, u32[]{:S(2)}) %collective-permute-start.13) | collective-permute-done | bytes 56192 | tf_op jit(solution)/shard_map/ppermute | solution.py:23
  232.2 3.4 %fusion.17 = f32[3,32,16,128]{3,2,1,0:T(8,128)} fusion(f32[3,32,16,128]{3,2,1,0:T(8,128)S(1)} %fusion.60, f32[6,32,18,1]{3,2,1,0:T(8,128)S(1)} %copy-done.4, f32[6,32,1,128]{3,2,1,0:T(1,128)S(1)} %collective-permute-done.10, f32[6,32,1,128]{3,2,1,0:T(1,128)S(1)} %copy-done.18, f32[3,32,16,128]{3,2,1,0:T(8,128)S(1)} %get-tuple-element.54, ...), kind=kLoop, calls=%fused_computation.58 | loop fusion | flops 7077888 | bytes 3482304 | tf_op jit(solution)/shard_map/sub | solution.py:107
  (171 shorter events, 66.2 us)
Async XLA Ops:
  7.2 63.0 %reduce-scatter.2.cloned.1.call-start = ((), (), s32[]{:S(2)}) async-start(), calls=%async_computation.1 | async-start | bytes 278528 | tf_op jit(solution)/shard_map/reduce_scatter | solution.py:85
  10.2 6.7 %collective-permute-start.18 = (f32[3,32,1,128]{3,2,1,0:T(1,128)S(1)}, f32[3,32,1,128]{3,2,1,0:T(1,128)S(1)}, u32[]{:S(2)}, u32[]{:S(2)}) collective-permute-start(f32[3,32,1,128]{3,2,1,0:T(1,128)S(1)} %get-tuple-element.51), channel_id=1, source_target_pairs={{0,8},{8,16},{16,24},{1,9},{9,17},{17,25},{2,10},{10,18},{18,26},{... | collective-permute-start | bytes 147464 | tf_op jit(solution)/shard_map/ppermute | solution.py:20
  15.2 6.0 %collective-permute-start.19 = (f32[3,32,1,128]{3,2,1,0:T(1,128)S(1)}, f32[3,32,1,128]{3,2,1,0:T(1,128)S(1)}, u32[]{:S(2)}, u32[]{:S(2)}) collective-permute-start(f32[3,32,1,128]{3,2,1,0:T(1,128)S(1)} %get-tuple-element.52), channel_id=1, source_target_pairs={{8,0},{16,8},{24,16},{9,1},{17,9},{25,17},{10,2},{18,10},{26,18},{... | collective-permute-start | bytes 147464 | tf_op jit(solution)/shard_map/ppermute | solution.py:23
  79.2 17.4 %collective-permute-start = (f32[6,32,1,128]{3,2,1,0:T(1,128)S(1)}, f32[6,32,1,128]{3,2,1,0:T(1,128)S(1)}, u32[]{:S(2)}, u32[]{:S(2)}) collective-permute-start(f32[6,32,1,128]{3,2,1,0:T(1,128)S(1)} %get-tuple-element.43), channel_id=1, source_target_pairs={{0,8},{8,16},{16,24},{1,9},{9,17},{17,25},{2,10},{10,18},{18,26},{... | collective-permute-start | bytes 294920 | tf_op jit(solution)/shard_map/ppermute | solution.py:20
  82.7 14.0 %collective-permute-start.1 = (f32[6,32,1,128]{3,2,1,0:T(1,128)S(1)}, f32[6,32,1,128]{3,2,1,0:T(1,128)S(1)}, u32[]{:S(2)}, u32[]{:S(2)}) collective-permute-start(f32[6,32,1,128]{3,2,1,0:T(1,128)S(1)} %get-tuple-element.44), channel_id=1, source_target_pairs={{8,0},{16,8},{24,16},{9,1},{17,9},{25,17},{10,2},{18,10},{26,18},{... | collective-permute-start | bytes 294920 | tf_op jit(solution)/shard_map/ppermute | solution.py:23
  90.3 4.8 %collective-permute-start.21 = (f32[3,32,18,1]{1,3,2,0:T(1,128)S(1)}, f32[3,32,18,1]{1,3,2,0:T(1,128)S(1)}, u32[]{:S(2)}, u32[]{:S(2)}) collective-permute-start(f32[3,32,18,1]{1,3,2,0:T(1,128)S(1)} %copy.26), channel_id=1, source_target_pairs={{2,0},{4,2},{6,4},{3,1},{5,3},{7,5},{10,8},{12,10},{14,12},{11,9},... | collective-permute-start | bytes 20744 | tf_op jit(solution)/shard_map/ppermute | solution.py:23
  102.3 13.5 %collective-permute-start.2 = (f32[6,32,18,1]{1,3,2,0:T(1,128)S(1)}, f32[6,32,18,1]{1,3,2,0:T(1,128)S(1)}, u32[]{:S(2)}, u32[]{:S(2)}) collective-permute-start(f32[6,32,18,1]{1,3,2,0:T(1,128)S(1)} %copy.12), channel_id=1, source_target_pairs={{0,2},{2,4},{4,6},{1,3},{3,5},{5,7},{8,10},{10,12},{12,14},{9,11},... | collective-permute-start | bytes 41480 | tf_op jit(solution)/shard_map/ppermute | solution.py:20
  109.1 9.0 %collective-permute-start.3 = (f32[6,32,18,1]{1,3,2,0:T(1,128)S(1)}, f32[6,32,18,1]{1,3,2,0:T(1,128)S(1)}, u32[]{:S(2)}, u32[]{:S(2)}) collective-permute-start(f32[6,32,18,1]{1,3,2,0:T(1,128)S(1)} %copy.13), channel_id=1, source_target_pairs={{2,0},{4,2},{6,4},{3,1},{5,3},{7,5},{10,8},{12,10},{14,12},{11,9},... | collective-permute-start | bytes 41480 | tf_op jit(solution)/shard_map/ppermute | solution.py:23
  112.0 15.2 %collective-permute-start.22 = (f32[3,1,18,130]{3,2,1,0:T(8,128)S(1)}, f32[3,1,18,130]{3,2,1,0:T(8,128)S(1)}, u32[]{:S(2)}, u32[]{:S(2)}) collective-permute-start(f32[3,1,18,130]{3,2,1,0:T(8,128)S(1)} %get-tuple-element.36), channel_id=1, source_target_pairs={{0,1},{2,3},{4,5},{6,7},{8,9},{10,11},{12,13},{14,15},{16,17},{18,... | collective-permute-start | bytes 84248 | tf_op jit(solution)/shard_map/ppermute | solution.py:20
  114.5 34.3 %collective-permute-start.26 = (f32[3,1,18,130]{3,2,1,0:T(8,128)}, f32[3,1,18,130]{3,2,1,0:T(8,128)}, u32[]{:S(2)}, u32[]{:S(2)}) collective-permute-start(f32[3,1,18,130]{3,2,1,0:T(8,128)} %get-tuple-element.35), channel_id=1, source_target_pairs={{1,0},{3,2},{5,4},{7,6},{9,8},{11,10},{13,12},{15,14},{17,16},{19,... | collective-permute-start | bytes 84248 | tf_op jit(solution)/shard_map/ppermute | solution.py:23
  121.8 10.2 %collective-permute-start.5 = (f32[6,1,18,130]{3,2,1,0:T(8,128)S(1)}, f32[6,1,18,130]{3,2,1,0:T(8,128)S(1)}, u32[]{:S(2)}, u32[]{:S(2)}) collective-permute-start(f32[6,1,18,130]{3,2,1,0:T(8,128)S(1)} %get-tuple-element.32), channel_id=1, source_target_pairs={{0,1},{2,3},{4,5},{6,7},{8,9},{10,11},{12,13},{14,15},{16,17},{18,... | collective-permute-start | bytes 168488 | tf_op jit(solution)/shard_map/ppermute | solution.py:20
  128.1 5.6 %collective-permute-start.24 = (f32[32,16,1]{2,1,0:T(8,128)S(1)}, f32[32,16,1]{2,1,0:T(8,128)S(1)}, u32[]{:S(2)}, u32[]{:S(2)}) collective-permute-start(f32[32,16,1]{2,1,0:T(8,128)S(1)} %bitcast.50), channel_id=1, source_target_pairs={{2,0},{4,2},{6,4},{3,1},{5,3},{7,5},{10,8},{12,10},{14,12},{11,9},... | collective-permute-start | bytes 6152 | tf_op jit(solution)/shard_map/ppermute | solution.py:12
  129.4 8.1 %collective-permute-start.23 = (f32[32,1,128]{2,1,0:T(1,128)S(1)}, f32[32,1,128]{2,1,0:T(1,128)S(1)}, u32[]{:S(2)}, u32[]{:S(2)}) collective-permute-start(f32[32,1,128]{2,1,0:T(1,128)S(1)} %slice.551), channel_id=1, source_target_pairs={{8,0},{16,8},{24,16},{9,1},{17,9},{25,17},{10,2},{18,10},{26,18},{... | collective-permute-start | bytes 49160 | tf_op jit(solution)/shard_map/ppermute | solution.py:12
  130.7 5.5 %collective-permute-start.25 = (f32[1,16,128]{2,1,0:T(8,128)S(1)}, f32[1,16,128]{2,1,0:T(8,128)S(1)}, u32[]{:S(2)}, u32[]{:S(2)}) collective-permute-start(f32[1,16,128]{2,1,0:T(8,128)S(1)} %slice.555), channel_id=1, source_target_pairs={{1,0},{3,2},{5,4},{7,6},{9,8},{11,10},{13,12},{15,14},{17,16},{19,... | collective-permute-start | bytes 24584 | tf_op jit(solution)/shard_map/ppermute | solution.py:12
  132.4 7.0 %collective-permute-start.7 = (f32[32,16,1]{2,1,0:T(8,128)S(1)}, f32[32,16,1]{2,1,0:T(8,128)S(1)}, u32[]{:S(2)}, u32[]{:S(2)}) collective-permute-start(f32[32,16,1]{2,1,0:T(8,128)S(1)} %bitcast.48), channel_id=1, source_target_pairs={{2,0},{4,2},{6,4},{3,1},{5,3},{7,5},{10,8},{12,10},{14,12},{11,9},... | collective-permute-start | bytes 6152 | tf_op jit(solution)/shard_map/ppermute | solution.py:12
  133.7 8.1 %collective-permute-start.6 = (f32[32,1,128]{2,1,0:T(1,128)S(1)}, f32[32,1,128]{2,1,0:T(1,128)S(1)}, u32[]{:S(2)}, u32[]{:S(2)}) collective-permute-start(f32[32,1,128]{2,1,0:T(1,128)S(1)} %slice.530), channel_id=1, source_target_pairs={{8,0},{16,8},{24,16},{9,1},{17,9},{25,17},{10,2},{18,10},{26,18},{... | collective-permute-start | bytes 49160 | tf_op jit(solution)/shard_map/ppermute | solution.py:12
  136.2 5.5 %collective-permute-start.8 = (f32[1,16,128]{2,1,0:T(8,128)S(1)}, f32[1,16,128]{2,1,0:T(8,128)S(1)}, u32[]{:S(2)}, u32[]{:S(2)}) collective-permute-start(f32[1,16,128]{2,1,0:T(8,128)S(1)} %slice.534), channel_id=1, source_target_pairs={{1,0},{3,2},{5,4},{7,6},{9,8},{11,10},{13,12},{15,14},{17,16},{19,... | collective-permute-start | bytes 24584 | tf_op jit(solution)/shard_map/ppermute | solution.py:12
  137.7 8.3 %collective-permute-start.4 = (f32[6,1,18,130]{3,2,1,0:T(8,128)S(1)}, f32[6,1,18,130]{3,2,1,0:T(8,128)S(1)}, u32[]{:S(2)}, u32[]{:S(2)}) collective-permute-start(f32[6,1,18,130]{3,2,1,0:T(8,128)S(1)} %get-tuple-element.31), channel_id=1, source_target_pairs={{1,0},{3,2},{5,4},{7,6},{9,8},{11,10},{13,12},{15,14},{17,16},{19,... | collective-permute-start | bytes 168488 | tf_op jit(solution)/shard_map/ppermute | solution.py:23
  153.2 13.5 %collective-permute-start.27 = (f32[3,32,1,128]{3,2,1,0:T(1,128)S(1)}, f32[3,32,1,128]{3,2,1,0:T(1,128)S(1)}, u32[]{:S(2)}, u32[]{:S(2)}) collective-permute-start(f32[3,32,1,128]{3,2,1,0:T(1,128)S(1)} %get-tuple-element.49), channel_id=1, source_target_pairs={{0,8},{8,16},{16,24},{1,9},{9,17},{17,25},{2,10},{10,18},{18,26},{... | collective-permute-start | bytes 147464 | tf_op jit(solution)/shard_map/ppermute | solution.py:20
  158.4 8.4 %collective-permute-start.28 = (f32[3,32,1,128]{3,2,1,0:T(1,128)S(1)}, f32[3,32,1,128]{3,2,1,0:T(1,128)S(1)}, u32[]{:S(2)}, u32[]{:S(2)}) collective-permute-start(f32[3,32,1,128]{3,2,1,0:T(1,128)S(1)} %get-tuple-element.50), channel_id=1, source_target_pairs={{8,0},{16,8},{24,16},{9,1},{17,9},{25,17},{10,2},{18,10},{26,18},{... | collective-permute-start | bytes 147464 | tf_op jit(solution)/shard_map/ppermute | solution.py:23
  160.0 21.1 %collective-permute-start.10 = (f32[6,32,1,128]{3,2,1,0:T(1,128)S(1)}, f32[6,32,1,128]{3,2,1,0:T(1,128)S(1)}, u32[]{:S(2)}, u32[]{:S(2)}) collective-permute-start(f32[6,32,1,128]{3,2,1,0:T(1,128)S(1)} %get-tuple-element.42), channel_id=1, source_target_pairs={{8,0},{16,8},{24,16},{9,1},{17,9},{25,17},{10,2},{18,10},{26,18},{... | collective-permute-start | bytes 294920 | tf_op jit(solution)/shard_map/ppermute | solution.py:23
  161.3 19.8 %collective-permute-start.9 = (f32[6,32,1,128]{3,2,1,0:T(1,128)S(1)}, f32[6,32,1,128]{3,2,1,0:T(1,128)S(1)}, u32[]{:S(2)}, u32[]{:S(2)}) collective-permute-start(f32[6,32,1,128]{3,2,1,0:T(1,128)S(1)} %get-tuple-element.41), channel_id=1, source_target_pairs={{0,8},{8,16},{16,24},{1,9},{9,17},{17,25},{2,10},{10,18},{18,26},{... | collective-permute-start | bytes 294920 | tf_op jit(solution)/shard_map/ppermute | solution.py:20
  173.5 6.1 %collective-permute-start.30 = (f32[3,32,18,1]{1,3,2,0:T(1,128)S(1)}, f32[3,32,18,1]{1,3,2,0:T(1,128)S(1)}, u32[]{:S(2)}, u32[]{:S(2)}) collective-permute-start(f32[3,32,18,1]{1,3,2,0:T(1,128)S(1)} %copy.31), channel_id=1, source_target_pairs={{2,0},{4,2},{6,4},{3,1},{5,3},{7,5},{10,8},{12,10},{14,12},{11,9},... | collective-permute-start | bytes 20744 | tf_op jit(solution)/shard_map/ppermute | solution.py:23
  187.5 18.1 %collective-permute-start.11 = (f32[6,32,18,1]{1,3,2,0:T(1,128)}, f32[6,32,18,1]{1,3,2,0:T(1,128)}, u32[]{:S(2)}, u32[]{:S(2)}) collective-permute-start(f32[6,32,18,1]{1,3,2,0:T(1,128)} %copy.18), channel_id=1, source_target_pairs={{0,2},{2,4},{4,6},{1,3},{3,5},{5,7},{8,10},{10,12},{12,14},{9,11},... | collective-permute-start | bytes 41480 | tf_op jit(solution)/shard_map/ppermute | solution.py:20
  195.5 13.1 %collective-permute-start.12 = (f32[6,32,18,1]{1,3,2,0:T(1,128)}, f32[6,32,18,1]{1,3,2,0:T(1,128)}, u32[]{:S(2)}, u32[]{:S(2)}) collective-permute-start(f32[6,32,18,1]{1,3,2,0:T(1,128)} %copy.19), channel_id=1, source_target_pairs={{2,0},{4,2},{6,4},{3,1},{5,3},{7,5},{10,8},{12,10},{14,12},{11,9},... | collective-permute-start | bytes 41480 | tf_op jit(solution)/shard_map/ppermute | solution.py:23
  198.5 16.3 %collective-permute-start.31 = (f32[3,1,18,130]{3,2,1,0:T(8,128)}, f32[3,1,18,130]{3,2,1,0:T(8,128)}, u32[]{:S(2)}, u32[]{:S(2)}) collective-permute-start(f32[3,1,18,130]{3,2,1,0:T(8,128)} %get-tuple-element.33), channel_id=1, source_target_pairs={{1,0},{3,2},{5,4},{7,6},{9,8},{11,10},{13,12},{15,14},{17,16},{19,... | collective-permute-start | bytes 84248 | tf_op jit(solution)/shard_map/ppermute | solution.py:23
  199.8 15.0 %collective-permute-start.32 = (f32[3,1,18,130]{3,2,1,0:T(8,128)}, f32[3,1,18,130]{3,2,1,0:T(8,128)}, u32[]{:S(2)}, u32[]{:S(2)}) collective-permute-start(f32[3,1,18,130]{3,2,1,0:T(8,128)} %get-tuple-element.34), channel_id=1, source_target_pairs={{0,1},{2,3},{4,5},{6,7},{8,9},{10,11},{12,13},{14,15},{16,17},{18,... | collective-permute-start | bytes 84248 | tf_op jit(solution)/shard_map/ppermute | solution.py:20
  213.2 5.7 %collective-permute-start.14 = (f32[6,1,18,130]{3,2,1,0:T(8,128)S(1)}, f32[6,1,18,130]{3,2,1,0:T(8,128)S(1)}, u32[]{:S(2)}, u32[]{:S(2)}) collective-permute-start(f32[6,1,18,130]{3,2,1,0:T(8,128)S(1)} %get-tuple-element.30), channel_id=1, source_target_pairs={{0,1},{2,3},{4,5},{6,7},{8,9},{10,11},{12,13},{14,15},{16,17},{18,... | collective-permute-start | bytes 168488 | tf_op jit(solution)/shard_map/ppermute | solution.py:20
  219.2 6.1 %collective-permute-start.16 = (f32[32,16,1]{2,1,0:T(8,128)S(1)}, f32[32,16,1]{2,1,0:T(8,128)S(1)}, u32[]{:S(2)}, u32[]{:S(2)}) collective-permute-start(f32[32,16,1]{2,1,0:T(8,128)S(1)} %bitcast.49), channel_id=1, source_target_pairs={{2,0},{4,2},{6,4},{3,1},{5,3},{7,5},{10,8},{12,10},{14,12},{11,9},... | collective-permute-start | bytes 6152 | tf_op jit(solution)/shard_map/ppermute | solution.py:12
  220.5 6.8 %collective-permute-start.15 = (f32[32,1,128]{2,1,0:T(1,128)S(1)}, f32[32,1,128]{2,1,0:T(1,128)S(1)}, u32[]{:S(2)}, u32[]{:S(2)}) collective-permute-start(f32[32,1,128]{2,1,0:T(1,128)S(1)} %slice.543), channel_id=1, source_target_pairs={{8,0},{16,8},{24,16},{9,1},{17,9},{25,17},{10,2},{18,10},{26,18},{... | collective-permute-start | bytes 49160 | tf_op jit(solution)/shard_map/ppermute | solution.py:12
  221.8 5.5 %collective-permute-start.17 = (f32[1,16,128]{2,1,0:T(8,128)S(1)}, f32[1,16,128]{2,1,0:T(8,128)S(1)}, u32[]{:S(2)}, u32[]{:S(2)}) collective-permute-start(f32[1,16,128]{2,1,0:T(8,128)S(1)} %slice.547), channel_id=1, source_target_pairs={{1,0},{3,2},{5,4},{7,6},{9,8},{11,10},{13,12},{15,14},{17,16},{19,... | collective-permute-start | bytes 24584 | tf_op jit(solution)/shard_map/ppermute | solution.py:12
  223.8 8.3 %collective-permute-start.13 = (f32[6,1,18,130]{3,2,1,0:T(8,128)S(1)}, f32[6,1,18,130]{3,2,1,0:T(8,128)S(1)}, u32[]{:S(2)}, u32[]{:S(2)}) collective-permute-start(f32[6,1,18,130]{3,2,1,0:T(8,128)S(1)} %get-tuple-element.29), channel_id=1, source_target_pairs={{1,0},{3,2},{5,4},{7,6},{9,8},{11,10},{13,12},{15,14},{17,16},{19,... | collective-permute-start | bytes 168488 | tf_op jit(solution)/shard_map/ppermute | solution.py:23
  (36 other events, 585.1 us)
Sparse Core Ops, SparseCore 0:
  12.1 57.9 reduce-scatter.1
where the time goes:
time: 245 us; the launch traced here: 242 us
  waiting for transfers between devices  74.1 us (30%)
  starting transfers between devices  73.9 us (30%)
  local copies, waits for them, and re-layouts  45.8 us (19%)
  other arithmetic  24 us (10%)
  between operations  15 us (6%)
  blocking collectives  8.78 us (4%)
    reduce_scatter x1, waiting for transfers between devices, shards(): lax.psum_scatter(spread, ('gx', 'gy'), scatter_dimension=0, tiled=True)  47.8 us
    ppermute x12, starting transfers between devices, extended(): lax.ppermute(lax.slice_in_dim(block, block.shape[dim] - width, None, axis...  46.5 us
    ppermute x12, waiting for transfers between devices, extended(): lax.ppermute(lax.slice_in_dim(block, 0, width, axis=dim), axis, backward)  18.3 us
    slice x7, local copies, waits for them, and re-layouts, extended(): lax.slice_in_dim(block, 0, width, axis=dim)  16.2 us
    ppermute x12, starting transfers between devices, extended(): lax.ppermute(lax.slice_in_dim(block, 0, width, axis=dim), axis, backward)  15.7 us
    slice x7, local copies, waits for them, and re-layouts, extended(): lax.slice_in_dim(block, block.shape[dim] - width, None, axis=dim)  11.8 us
    ppermute x9, starting transfers between devices, shifted(): return lax.ppermute(value, axis, pairs)  11.6 us
    psum x1, blocking collectives, shards(): forcing = lax.psum(forcing, 'gz')  8.78 us
  transfers between devices with their start and end apart: 34, of which 11 were waited for; matrix products, arithmetic and copies ran while one was open for 20% of the time, Pallas kernels for 0%

commit v1 on v0

v1 whole, which is shorter than its diff:
```python
import functools

import jax
import jax.numpy as jnp
from jax import lax
from jax.experimental import pallas as pl
from jax.experimental.pallas import tpu as pltpu
from jax.sharding import PartitionSpec as P

STEPS = 2
W = 2
COLS = 3 * W
FIELDS = 9
AXES = ("gx", "gy", "gz")


def mate(index, count, second):
    other = index + 1 if (index + second) % 2 == 0 else index - 1
    return other if 0 <= other < count else index


def exchange(value, shape, partner):
    nx, ny, nz = shape
    pairs = []
    for i in range(nx):
        for j in range(ny):
            for k in range(nz):
                a, b, c = partner(i, j, k)
                pairs.append(((i * ny + j) * nz + k, (a * ny + b) * nz + c))
    return lax.ppermute(value, AXES, pairs)


def even(index):
    return lax.rem(index, 2) == 0


VM = pl.BlockSpec(memory_space=pltpu.VMEM)
HBM = pl.BlockSpec(memory_space=pltpu.HBM)
PARAMS = pltpu.CompilerParams(vmem_limit_bytes=40 * 1024 * 1024)


def struct(*shape):
    return jax.ShapeDtypeStruct(shape, jnp.float32)


BASE = 8
EDGE_ROWS = 8 * -(-FIELDS * W * W // 8)


def rows_of(dims):
    cz, cx, _ = dims
    return cz + 2 * W + 1, cx + 2 * BASE, cx + 8


def pack_kernel(vel, pres, mod, av, ap, values, owner, line, step, fields, xa, xb, za, zb, xza, xzb, xzc, xzd, sens, *scratch, dims):
    cz, cx, cy = dims
    own, inputs, sem = scratch[0], scratch[1:4], scratch[4]
    rows = own.shape[0]
    ex, ez = even(lax.axis_index("gx")), even(lax.axis_index("gz"))
    copies = [
        (vel, fields.at[pl.ds(0, 3)]),
        (pres, fields.at[3]),
        (mod, fields.at[4]),
        (av, fields.at[pl.ds(5, 3)]),
        (ap, fields.at[8]),
        (values, own),
        (owner, inputs[0]),
        (line, inputs[1]),
        (step, inputs[2]),
    ]
    copies = [pltpu.make_async_copy(a, b, sem.at[i]) for i, (a, b) in enumerate(copies)]
    for copy in copies:
        copy.start()
    for copy in copies[5:]:
        copy.wait()
    first_row = [inputs[i][...] for i in range(3)]
    code = first_row[0] * (STEPS * cx) + first_row[2] * cx + first_row[1]
    sens[0:rows, :] = own[...]
    sens[rows:rows + 8, :] = jnp.zeros((8, cy), jnp.float32)
    sens[rows:rows + 1, 0:rows] = code.astype(jnp.float32)
    x_rows, z_rows = FIELDS * W * cz, FIELDS * W * cx
    for face, at in ((xa, x_rows), (za, z_rows), (xza, EDGE_ROWS)):
        face[at:at + rows + 8, :] = sens[...]
    for copy in copies[:5]:
        copy.wait()
    for f in range(FIELDS):
        for l in range(W):
            first = fields[f, pl.ds(l, cz, stride=cx), :]
            last = fields[f, pl.ds(cx - W + l, cz, stride=cx), :]
            a = jnp.where(ex, last, first)
            b = jnp.where(ex, first, last)
            xa[pl.ds((f * W + l) * cz, cz), :] = a
            xb[pl.ds((f * W + l) * cz, cz), :] = b
            for x, (near, far) in ((a, (xza, xzc)), (b, (xzb, xzd))):
                near[pl.ds((f * W + l) * W, W), :] = jnp.where(ez, x[cz - W:], x[:W])
                if far is not None:
                    far[pl.ds((f * W + l) * W, W), :] = jnp.where(ez, x[:W], x[cz - W:])
            low = fields[f, pl.ds(l * cx, cx), :]
            high = fields[f, pl.ds((cz - W + l) * cx, cx), :]
            za[pl.ds((f * W + l) * cx, cx), :] = jnp.where(ez, high, low)
            if zb is not None:
                zb[pl.ds((f * W + l) * cx, cx), :] = jnp.where(ez, low, high)


def join_kernel(*refs):
    *ins, out = refs
    rows = out.shape[0] // len(ins)
    for i, ref in enumerate(ins):
        out[i * rows:(i + 1) * rows, :] = ref[ref.shape[0] - rows:, :]


def fill(ext, depths, edges, fields, xs, zs, xzs, dims, place):
    cz, cx, cy = dims
    _, wide, _ = rows_of(dims)
    (ix, nx), _, (iz, nz) = place
    ex, ez = even(ix), even(iz)
    has = {"xl": ix > 0, "xh": ix < nx - 1, "zl": iz > 0, "zh": iz < nz - 1}

    def sides(pair, parity, low, high):
        a, b = pair
        below = jnp.where(parity, 0.0 if b is None else b, a)
        above = jnp.where(parity, a, 0.0 if b is None else b)
        return jnp.where(low, below, 0.0), jnp.where(high, above, 0.0)

    for f in range(FIELDS):
        for plane in range(cz):
            ext[f, pl.ds((plane + W) * wide + BASE, cx), :] = fields[f, pl.ds(plane * cx, cx), :]
        depths[f, pl.ds(W * cx, (8 - 2 * W) * cx), :] = jnp.zeros(((8 - 2 * W) * cx, cy), jnp.float32)
        for l in range(W):
            n = f * W + l
            low, high = sides([x[pl.ds(n * cz, cz), :] for x in xs], ex, has["xl"], has["xh"])
            ext[f, pl.ds(W * wide + BASE + cx + l, cz, stride=wide), :] = high
            ext[f, pl.ds(W * wide + BASE - W + l, cz, stride=wide), :] = low
            low, high = sides([None if z is None else z[pl.ds(n * cx, cx), :] for z in zs], ez, has["zl"], has["zh"])
            ext[f, pl.ds(l * wide + BASE, cx), :] = low
            ext[f, pl.ds((cz + W + l) * wide + BASE, cx), :] = high
            depths[f, pl.ds((8 - W + l) * cx, cx), :] = low
            depths[f, pl.ds(l * cx, cx), :] = high
            got = [None if c is None else c[pl.ds(n * W, W), :] for c in xzs]
            near = sides(got[:2], ex, has["xl"], has["xh"])
            far = sides(got[2:], ex, has["xl"], has["xh"]) if got[2] is not None else (None, None)
            for part, row in ((0, BASE - W + l), (1, BASE + cx + l)):
                low, high = sides((near[part], far[part]), ez, has["zl"], has["zh"])
                edges[f, part * W + l] = jnp.concatenate([high, jnp.zeros((8 - 2 * W, cy), jnp.float32), low])
                for k in range(W):
                    ext[f, pl.ds(k * wide + row, 1), :] = low[k:k + 1]
                    ext[f, pl.ds((cz + W + k) * wide + row, 1), :] = high[k:k + 1]


def lane_of(shape):
    return lax.broadcasted_iota(jnp.int32, shape, 1)


def roll(value, by, axis):
    size = value.shape[axis]
    return pltpu.roll(value, by % size, axis)


def add_strips(low, high, row, x, cy):
    at = COLS * (x + W)
    lane = lane_of(row.shape)
    low = jnp.where(lane >= at + W, roll(row, at + W, 1), low)
    high = jnp.where(lane >= at, roll(row, at - (cy - 2 * W), 1), high)
    return low, high


def strip_kernel(fields, xa, xb, za, zb, xza, xzb, xzc, xzd, ext, strips, ya, yb, depths, edges, *, dims, counts):
    cz, cx, cy = dims
    _, wide, _ = rows_of(dims)
    planes = cz + 8
    place = [(lax.axis_index(a), n) for a, n in zip(AXES, counts)]
    fill(ext, depths, edges, fields, (xa, xb), (za, zb), (xza, xzb, xzc, xzd), dims, place)
    ey = even(place[1][0])
    lane = lane_of((planes, cy))
    middle = (lane % COLS >= W) & (lane % COLS < 2 * W)
    for g in range(FIELDS // 3):
        outs = [jnp.zeros((planes, cy), jnp.float32)] * 2
        for j in range(3):
            f = 3 * g + j
            low = jnp.zeros((planes, cy), jnp.float32)
            high = jnp.zeros((planes, cy), jnp.float32)
            for x in range(-W, cx + W):
                own = ext[f, pl.ds(W * wide + BASE + x, cz, stride=wide), :]
                if 0 <= x < cx:
                    beyond = depths[f, pl.ds(x, 8, stride=cx), :]
                else:
                    beyond = edges[f, x + W if x < 0 else x - cx + W]
                low, high = add_strips(low, high, jnp.concatenate([own, beyond]), x, cy)
            strips[f, 0] = low
            strips[f, 1] = high
            for n, (odd_side, even_side) in enumerate(((low, high), (high, low))):
                mine = jnp.where(middle, jnp.where(ey, even_side, odd_side), 0.0)
                outs[n] = outs[n] + roll(mine, W * (j - 1), 1)
        ya[g] = outs[0]
        yb[g] = outs[1]


def lines_kernel(own_rows, far_rows, ya, yb, *refs, dims, counts, rows, joined):
    _, cx, cy = dims
    nx, ny, _ = counts
    _, _, wide = rows_of(dims)
    outs, dense = refs[:ny], refs[ny]
    ix, iy = lax.axis_index("gx"), lax.axis_index("gy")
    size = rows + 8
    ins = [(ref, i * size) for ref in (own_rows, far_rows) if ref is not None for i in range(ref.shape[0] // size)]
    values = jnp.concatenate([r[at:at + rows, :] for r, at in ins], axis=0)
    code = jnp.concatenate([r[at + rows:at + rows + 1, 0:rows] for r, at in ins], axis=1).astype(jnp.int32)
    owner, rest = code // (STEPS * cx), code % (STEPS * cx)
    step, line = rest // cx, rest % cx
    ox, oy = owner // ny, owner % ny
    row = (ox - ix) * cx + line + W
    key = jnp.where((row >= 0) & (row < cx + 2 * W), (oy * STEPS + step) * wide + row, -1)
    table = lax.broadcasted_iota(jnp.int32, (ny * STEPS * wide, len(ins) * rows), 0) == key
    spread = jnp.dot(
        table.astype(jnp.float32), values, precision=lax.Precision.HIGHEST, preferred_element_type=jnp.float32
    )
    block = STEPS * wide
    dense[0] = jnp.zeros((block, cy), jnp.float32)
    dense[ny + 1] = jnp.zeros((block, cy), jnp.float32)
    for b in range(ny):
        dense[b + 1] = spread[b * block:(b + 1) * block]
    lane = lane_of((1, cy))
    for k in range(ny):
        out, base = outs[k], 0
        if k in joined:
            strip = (ya, yb)[joined.index(k)]
            base = strip.shape[0] * strip.shape[1]
            out[0:base, :] = strip[...].reshape(base, cy)
        at = lax.bitwise_xor(iy, k)
        own, below, above = dense[at + 1], dense[at], dense[at + 2]
        out[base:base + block, :] = own
        out[base + block:base + block + 8, :] = jnp.zeros((8, cy), jnp.float32)
        for s in range(STEPS):
            low = jnp.zeros((1, cy), jnp.float32)
            high = jnp.zeros((1, cy), jnp.float32)
            for x in range(-W, cx + W):
                r = s * wide + x + W
                start = COLS * (x + W)
                low = jnp.where(lane >= start, roll(below[r:r + 1], start - (cy - W), 1), low)
                low, high = add_strips(low, high, own[r:r + 1], x, cy)
                high = jnp.where(lane >= start + 2 * W, roll(above[r:r + 1], start + 2 * W, 1), high)
            out[base + block + 2 * s:base + block + 2 * s + 1, :] = low
            out[base + block + 2 * s + 1:base + block + 2 * s + 2, :] = high


def strip_steps(s, mask, f1, f0):
    v, p, mod, av, ap = s[0:3], s[3], s[4], s[5:8], s[8]

    def keep(a):
        return jnp.where(mask, a, 0.0)

    def lap(a):
        total = roll(a, 1, 0) + roll(a, -1, 0) + roll(a, COLS, 1) + roll(a, -COLS, 1) + roll(a, 1, 1) + roll(a, -1, 1)
        return total - 6.0 * a

    def div(u):
        return (u[0] - roll(u[0], COLS, 1)) + (u[1] - roll(u[1], 1, 1)) + (u[2] - roll(u[2], 1, 0))

    def grad(q):
        return roll(q, -COLS, 1) - q, roll(q, -1, 1) - q, roll(q, -1, 0) - q

    b0 = [lap(a) for a in v]
    g = grad(keep(p + div(v)))
    v1 = [keep(v[c] + 0.25 * (g[c] + mod * b0[c])) for c in range(3)]
    av = [av[0], av[1], av[2] + f1]
    shear = sum(av[c] * lap(v1[c]) for c in range(3))
    m = keep(ap - 0.25 * div(av))
    g = grad(m)
    av = [keep(av[c] + 0.25 * lap(mod * av[c]) - g[c]) for c in range(3)]
    av = [av[0], av[1], av[2] + f0]
    shear = 0.25 * (shear + sum(av[c] * b0[c] for c in range(3)))
    m = keep(m - 0.25 * div(av))
    g = grad(m)
    av = [av[c] + 0.25 * lap(mod * av[c]) - g[c] for c in range(3)]
    return av + [m, shear]


def main_steps(ext, forced_z, force, outs, scratch, dims, place):
    cz, cx, cy = dims
    _, wide, short = rows_of(dims)
    (ix, nx), _, (iz, nz) = place
    out_v, out_p, out_s = outs
    w0, b0, v1, a1, w1, q1 = scratch

    row = lax.broadcasted_iota(jnp.int32, (short, cy), 0)
    inside1 = ((row > 0) & (row <= cx)) | ((row > cx) & (ix < nx - 1)) | ((row == 0) & (ix > 0))
    inside0 = (row < cx) | (ix < nx - 1)

    def keep(a, inside, plane):
        at = iz * cz + plane - W
        return jnp.where(inside & ((at >= 0) & (at < nz * cz)), a, 0.0)

    def lap(below, a, above, lower, upper):
        return (above + below) + (lower + upper) + (roll(a, 1, 1) + roll(a, -1, 1)) - 6.0 * a

    def wider(f, plane, dx=0):
        at = pl.ds(plane * wide + (BASE - 1 + dx), short)
        return forced_z[at, :] if f == 7 else ext[f, at, :]

    def weight(c, plane, dx=0):
        return w0[c, pl.ds(plane * wide + (BASE - 1 + dx), short), :]

    def weigh(plane):
        at = pl.ds(pl.multiple_of(plane * wide, 8), wide)
        for c in range(3):
            w0[c, at, :] = ext[4, at, :] * (forced_z[at, :] if c == 2 else ext[5 + c, at, :])

    def pressure(plane, base, q, scale):
        vx, vy, vz = (wider(base + c, plane) for c in range(3))
        d = (vx - wider(base, plane, -1)) + (vy - roll(vy, 1, 1)) + (vz - wider(base + 2, plane - 1))
        return keep(wider(q, plane) + scale * d, inside1, plane)

    def whole(plane):
        return pl.ds(pl.multiple_of(plane * short, 8), short)

    def first(plane, carry):
        p1, m = carry
        p1_above = pressure(plane + 1, 0, 3, 1.0)
        m_above = pressure(plane + 1, 5, 8, -0.25)
        q1[0, whole(plane + 1), :] = p1_above
        q1[1, whole(plane + 1), :] = m_above
        next_row = pl.ds(plane * short + 1, short)
        g = (q1[0, next_row, :] - p1, roll(p1, -1, 1) - p1, p1_above - p1)
        h = (q1[1, next_row, :] - m, roll(m, -1, 1) - m, m_above - m)
        mod = wider(4, plane)
        weigh(plane + 2)
        for c in range(3):
            v = wider(c, plane)
            bend = lap(wider(c, plane - 1), v, wider(c, plane + 1), wider(c, plane, -1), wider(c, plane, 1))
            b0[c, whole(plane), :] = bend
            v1[c, whole(plane), :] = keep(v + 0.25 * (g[c] + mod * bend), inside1, plane)
            a = wider(5 + c, plane)
            spring = lap(weight(c, plane - 1), weight(c, plane), weight(c, plane + 1), weight(c, plane, -1), weight(c, plane, 1))
            a = keep(a + 0.25 * spring - h[c], inside1, plane)
            if c == 2:
                a = a + jnp.where(plane == W, force[pl.ds(1, short), :], 0.0)
            a1[c, whole(plane), :] = a
            w1[c, whole(plane), :] = mod * a
        return p1_above, m_above

    for plane in range(3):
        weigh(plane)
    begin = (pressure(1, 0, 3, 1.0), pressure(1, 5, 8, -0.25))
    for i in range(2):
        q1[i, whole(1), :] = begin[i]
    lax.fori_loop(1, cz + W + 1, first, begin, unroll=2)

    def step(ref, c, plane, dx=0, count=cx):
        return ref[c, pl.ds(plane * short + (1 + dx), count), :]

    def pressure1(plane):
        ax, ay, az = (step(a1, c, plane, 0, short) for c in range(3))
        d = (ax - step(a1, 0, plane, -1, short)) + (ay - roll(ay, 1, 1)) + (az - step(a1, 2, plane - 1, 0, short))
        return keep(step(q1, 1, plane, 0, short) - 0.25 * d, inside0, plane)

    def second(plane, m):
        m_above = pressure1(plane + 1)
        q1[2, whole(plane + 1), :] = m_above
        m, above = m[:cx], m_above[:cx]
        h = (q1[2, pl.ds(plane * short + 1, cx), :] - m, roll(m, -1, 1) - m, above - m)
        own = pl.ds(pl.multiple_of((plane - W) * cx, 8), cx)
        shear = jnp.zeros((cx, cy), jnp.float32)
        for c in range(3):
            a = step(a1, c, plane)
            bend = lap(
                step(v1, c, plane - 1), step(v1, c, plane), step(v1, c, plane + 1), step(v1, c, plane, -1),
                step(v1, c, plane, 1),
            )
            spring = lap(
                step(w1, c, plane - 1), step(w1, c, plane), step(w1, c, plane + 1), step(w1, c, plane, -1),
                step(w1, c, plane, 1),
            )
            at = pl.ds(pl.multiple_of(plane * wide + BASE, 8), cx)
            at_first = forced_z[at, :] if c == 2 else ext[5 + c, at, :]
            shear = shear + (at_first * bend + a * step(b0, c, plane))
            out_v[c, own, :] = a + 0.25 * spring - h[c]
        out_p[own, :] = m
        out_s[own, :] = 0.25 * shear
        return m_above

    begin = pressure1(W)
    q1[2, whole(W), :] = begin
    lax.fori_loop(W, cz + W, second, begin, unroll=2)


def steps_kernel(ext, strips, *rest, dims, counts, lines, joined):
    cz, cx, cy = dims
    _, wide, short = rows_of(dims)
    planes = cz + 8
    forced = rest[:lines]
    out_v, out_p, out_s, force, forced_z, *scratch = rest[lines:]
    place = [(lax.axis_index(a), n) for a, n in zip(AXES, counts)]
    (ix, nx), (iy, ny), (iz, nz) = place
    block = STEPS * short
    size = block + 8
    total = forced[0][forced[0].shape[0] - size:, :]
    for ref in forced[1:]:
        total = total + ref[ref.shape[0] - size:, :]
    force[...] = jnp.where(iz == 0, total, 0.0)
    surface = pl.ds(W * wide + BASE - W, short)
    forced_z[...] = ext[7]
    forced_z[surface, :] = forced_z[surface, :] + force[pl.ds(short, short), :]
    main_steps(ext, forced_z, force, (out_v, out_p, out_s), scratch, dims, place)

    lane = lane_of((planes, cy))
    depth = lax.broadcasted_iota(jnp.int32, (planes, cy), 0)
    x, col = lane // COLS - W, lane % COLS
    z = jnp.where(depth < cz + W, depth, depth - planes)
    gx, gz = ix * cx + x, iz * cz + z
    solid = (x < cx + W) & (gx >= 0) & (gx < nx * cx) & (gz >= 0) & (gz < nz * cz)
    ey = even(iy)
    yfrom = [forced[k] for k in joined]
    results = []
    for side in range(2):
        s = []
        for f in range(FIELDS):
            g, j = f // 3, f % 3
            a, b = (ref[pl.ds(g * planes, planes), :] for ref in yfrom)
            if side == 0:
                fresh = jnp.where(iy > 0, roll(jnp.where(ey, b, a), -W * j, 1), 0.0)
                s.append(jnp.where(col < W, fresh, strips[f, 0]))
            else:
                fresh = jnp.where(iy < ny - 1, roll(jnp.where(ey, a, b), 2 * W - W * j, 1), 0.0)
                s.append(jnp.where(col >= 2 * W, fresh, strips[f, 1]))
        beyond = (col >= W) | (iy > 0) if side == 0 else (col < 2 * W) | (iy < ny - 1)
        top = depth == 0
        push = [jnp.where(top, force[pl.ds(block + 2 * t + side, 1), :], 0.0) for t in range(STEPS)]
        results.append(strip_steps(s, solid & beyond, push[1], push[0]))
    outs = [out_v.at[0], out_v.at[1], out_v.at[2], out_p, out_s]
    lane = lane_of((cz, cy))
    for low, high, ref in zip(*results, outs):
        low, high = low[:cz], high[:cz]
        for x0 in range(cx):
            start = COLS * (x0 + W)
            value = ref[pl.ds(x0, cz, stride=cx), :]
            value = jnp.where(lane < W, roll(low, -(start + W), 1), value)
            value = jnp.where(lane >= cy - W, roll(high, cy - W - (start + W), 1), value)
            ref[pl.ds(x0, cz, stride=cx), :] = value


def shards(vel, pres, modulus, adj_vel_in, adj_pres_in, sensor_values, sensor_owner, sensor_line, sensor_step):
    counts = tuple(lax.axis_size(a) for a in AXES)
    nx, ny, nz = counts
    dims = pres.shape
    cz, cx, cy = dims
    rows = sensor_values.shape[0]
    size = rows + 8
    planes, wide, short = rows_of(dims)
    deep = nz > 2

    x_rows, z_rows, edge_rows = FIELDS * W * cz, FIELDS * W * cx, EDGE_ROWS
    faces = [x_rows + size, x_rows, z_rows + size, z_rows if deep else None]
    faces += [edge_rows + size, edge_rows, edge_rows if deep else None, edge_rows if deep else None]
    spots = [i for i, n in enumerate(faces) if n is not None]

    def spread_out(refs):
        full = [None] * 8
        for i, ref in zip(spots, refs):
            full[i] = ref
        return full

    def pack(*refs):
        count = 10 + len(spots)
        pack_kernel(*refs[:10], *spread_out(refs[10:count]), *refs[count:], dims=dims)

    small = pltpu.VMEM((1, rows), jnp.int32)
    inputs = [
        vel.reshape(3, cz * cx, cy), pres.reshape(cz * cx, cy), modulus.reshape(cz * cx, cy),
        adj_vel_in.reshape(3, cz * cx, cy), adj_pres_in.reshape(cz * cx, cy), sensor_values,
        sensor_owner.reshape(1, rows), sensor_line.reshape(1, rows), sensor_step.reshape(1, rows),
    ]
    fields, *packed, sens = pl.pallas_call(
        pack, out_shape=[pltpu.VMEM((FIELDS, cz * cx, cy), jnp.float32)] + [struct(faces[i], cy) for i in spots] + [struct(size, cy)],
        in_specs=[HBM] * 9, out_specs=[VM] * (len(spots) + 2),
        scratch_shapes=[pltpu.VMEM((rows, cy), jnp.float32), small, small, small, pltpu.SemaphoreType.DMA((9,))],
        compiler_params=PARAMS, name="pack",
    )(*[pltpu.with_memory_space_constraint(x, pltpu.HBM) for x in inputs])
    seconds = [(0, None), (1, None), (None, 0), (None, 1), (0, 0), (1, 0), (0, 1), (1, 1)]

    def halo(value, sx, sz):
        def partner(i, j, k):
            return i if sx is None else mate(i, nx, sx), j, k if sz is None else mate(k, nz, sz)

        return exchange(value, counts, partner)

    halos = spread_out([halo(value, *seconds[i]) for i, value in zip(spots, packed)])

    parts = [sens, halos[0]] if deep else [sens, halos[0], halos[2], halos[4]]
    near = pl.pallas_call(
        join_kernel, out_shape=struct(len(parts) * size, cy), in_specs=[VM] * len(parts), out_specs=VM,
        compiler_params=PARAMS, name="join",
    )(*parts)
    far, reach = None, 2
    while reach < nx:
        if far is not None:
            near = jnp.concatenate([near, far])
        far = exchange(near, counts, lambda i, j, k, reach=reach: (i ^ reach, j, k))
        reach = 2 * reach

    depth = cz + 8
    y_face = struct(FIELDS // 3, depth, cy)

    def strip(own, *refs):
        count = len(spots)
        strip_kernel(own, *spread_out(refs[:count]), *refs[count:], dims=dims, counts=counts)

    ext, strips, ya, yb = pl.pallas_call(
        strip, out_shape=[pltpu.VMEM((FIELDS, planes * wide, cy), jnp.float32), struct(FIELDS, 2, depth, cy), y_face, y_face],
        in_specs=[VM] * (1 + len(spots)), out_specs=[VM] * 4,
        scratch_shapes=[pltpu.VMEM((FIELDS, 8 * cx, cy), jnp.float32), pltpu.VMEM((FIELDS, 2 * W, 8, cy), jnp.float32)],
        compiler_params=PARAMS, name="strip",
    )(fields, *[halos[i] for i in spots])

    second = ny - 1 if ny == 4 else ny
    joined = (1, second)
    line_rows = STEPS * short + 8
    strip_rows = FIELDS // 3 * depth

    def lines(*refs):
        if far is None:
            refs = refs[:1] + (None,) + refs[1:]
        lines_kernel(*refs, dims=dims, counts=counts, rows=rows, joined=joined)

    gathered = [near] if far is None else [near, far]
    forced = pl.pallas_call(
        lines, out_shape=[struct(line_rows + (strip_rows if k in joined else 0), cy) for k in range(ny)],
        in_specs=[VM] * (len(gathered) + 2), out_specs=[VM] * ny,
        scratch_shapes=[pltpu.VMEM((ny + 2, STEPS * short, cy), jnp.float32)], compiler_params=PARAMS, name="lines",
    )(*gathered, ya, yb)
    forced = [forced[0]] + [exchange(forced[k], counts, lambda i, j, m, k=k: (i, j ^ k, m)) for k in range(1, ny)]
    if second == ny:
        yb = exchange(yb, counts, lambda i, j, k: (i, mate(j, ny, 1), k))
    if deep:
        total = sum(f[f.shape[0] - line_rows:] for f in forced)
        total = lax.psum(total, "gz")
        forced = [total, jnp.concatenate([forced[1][:strip_rows], jnp.zeros_like(total)])] + (
            [jnp.concatenate([forced[3][:strip_rows], jnp.zeros_like(total)])] if second < ny else []
        )
        joined = (1, 2)
    if second == ny:
        joined = (1, len(forced))
        forced.append(jnp.concatenate([yb.reshape(strip_rows, cy), jnp.zeros((line_rows, cy), jnp.float32)]))

    def steps(*refs):
        steps_kernel(*refs, dims=dims, counts=counts, lines=len(forced), joined=joined)

    three = pltpu.VMEM((3, planes * short + 8, cy), jnp.float32)
    whole = pltpu.VMEM((planes * wide, cy), jnp.float32)
    out_v, out_p, out_s = pl.pallas_call(
        steps, out_shape=[struct(3, cz * cx, cy), struct(cz * cx, cy), struct(cz * cx, cy)],
        in_specs=[VM] * (2 + len(forced)), out_specs=[VM] * 3,
        scratch_shapes=[
            pltpu.VMEM((line_rows, cy), jnp.float32), whole, pltpu.VMEM((3, planes * wide, cy), jnp.float32),
            three, three, three, three, three,
        ],
        compiler_params=PARAMS, name="steps",
    )(ext, strips, *forced)
    return out_v.reshape(3, cz, cx, cy), out_p.reshape(cz, cx, cy), out_s.reshape(cz, cx, cy)


def solution(mesh):
    return jax.shard_map(
        shards,
        mesh=mesh,
        in_specs=(
            P(None, "gz", "gx", "gy"),
            P("gz", "gx", "gy"),
            P("gz", "gx", "gy"),
            P(None, "gz", "gx", "gy"),
            P("gz", "gx", "gy"),
            P(("gx", "gy", "gz"), None),
            P(("gx", "gy", "gz"), None),
            P(("gx", "gy", "gz")),
            P(("gx", "gy", "gz")),
        ),
        out_specs=(P(None, "gz", "gx", "gy"), P("gz", "gx", "gy"), P("gz", "gx", "gy")),
        check_vma=False,
    )
```

time: 245 us -> 40.8 us (0.17)
  waiting for transfers between devices: 74.1 us -> 9.44 us
  starting transfers between devices: 73.9 us -> 15.2 us
  local copies, waits for them, and re-layouts: 45.8 us -> 0 us
  other arithmetic: 24 us -> 0 us
  Pallas kernels: 0 us -> 15.3 us
  between operations: 15 us -> 0.69 us
  blocking collectives: 8.78 us -> 0 us
    ppermute x33 -> x9, starting transfers between devices: 73.8 us -> 15.2 us  [exchange(): return lax.ppermute(value, AXES, pairs)]
    reduce_scatter x1 -> x0, waiting for transfers between devices: 47.8 us -> none  [shards(): lax.psum_scatter(spread, ('gx', 'gy'), scatter_dimension=0, tiled=True)]
    slice x29 -> x0, local copies, waits for them, and re-layouts: 28.5 us -> none  [the longest x7 16.2 us: extended(): lax.slice_in_dim(block, 0, width, axis=dim)]
    ppermute x33 -> x9, waiting for transfers between devices: 26.2 us -> 9.44 us  [exchange(): return lax.ppermute(value, AXES, pairs)]
    ppermute x8 -> x0, local copies, waits for them, and re-layouts: 16.8 us -> none  [the longest x4 8.39 us: extended(): lax.ppermute(lax.slice_in_dim(block, block.shape[dim] - width, None, axis...]
    pallas_call x0 -> x5, Pallas kernels: none -> 15.3 us  [the longest x1 8.63 us: shards(): pl.pallas_call(steps, out_shape=[struct(3, cz * cx, cy), struct(cz * cx,...]
    psum x1 -> x0, blocking collectives: 8.78 us -> none  [shards(): forcing = lax.psum(forcing, 'gz')]
    sub x4 -> x0, other arithmetic: 6.76 us -> none  [the longest x2 6.18 us: shards(): lam_v = lam_v + 0.25 * weighted - 1.0 * gradient(middle)]
  transfers between devices with their start and end apart: 34 -> 9, of which waited for: 11 -> 3; matrix products, arithmetic and copies ran while one was open for 20% -> 0% of each run, Pallas kernels for 0% -> 9%
where the time goes in v1:
time: 40.8 us; the launch traced here: 40.6 us
  Pallas kernels  15.3 us (38%)
  starting transfers between devices  15.2 us (37%)
  waiting for transfers between devices  9.44 us (23%)
  between operations  0.69 us (2%)
    ppermute x9, starting transfers between devices, exchange(): return lax.ppermute(value, AXES, pairs)  15.2 us
    ppermute x9, waiting for transfers between devices, exchange(): return lax.ppermute(value, AXES, pairs)  9.44 us
    pallas_call x1, Pallas kernels, shards(): pl.pallas_call(steps, out_shape=[struct(3, cz * cx, cy), struct(cz * cx,...  8.63 us
    pallas_call x1, Pallas kernels, shards(): pl.pallas_call(strip, out_shape=[pltpu.VMEM((FIELDS, planes * wide, cy),...  3.66 us
    pallas_call x1, Pallas kernels, shards(): pl.pallas_call(pack, out_shape=[pltpu.VMEM((FIELDS, cz * cx, cy), jnp.flo...  1.86 us
    pallas_call x1, Pallas kernels, shards(): pl.pallas_call(lines, out_shape=[struct(line_rows + (strip_rows if k in j...  1.14 us
  transfers between devices with their start and end apart: 9, of which 3 were waited for; matrix products, arithmetic and copies ran while one was open for 0% of the time, Pallas kernels for 9%

profile of v1, /device:TPU:0, one launch (start us, length us, event | category | flops | bytes accessed | tf_op | source)
XLA Modules:
  0.0 40.6 jit_solution(12472297509295577457)
XLA Ops:
  0.6 1.9 %pack.1 = (f32[9,512,128]{2,1,0:T(8,128)S(1)}, f32[616,128]{1,0:T(8,128)S(1)}, f32[576,128]{1,0:T(8,128)S(1)}, f32[328,128]{1,0:T(8,128)S(1)}, f32[80,128]{1,0:T...) custom-call(f32[3,512,128]{2,1,0:T(8,128)} %bitcast.11, f32[512,128]{1,0:T(8,128)} %bitcast.13, ...), custom_call_target="tpu_custom_call" | custom-call | tf_op jit(solution)/shard_map/pack/pallas_call | solution.py:472
  2.5 3.1 %collective-permute-start = (f32[616,128]{1,0:T(8,128)S(1)}, f32[616,128]{1,0:T(8,128)S(1)}, u32[]{:S(2)}, u32[]{:S(2)}) collective-permute-start(f32[616,128]{1,0:T(8,128)S(1)} %get-tuple-element.22), channel_id=1, source_target_pairs={{0,8},{1,9},{2,10},{3,11},{4,12},{5,13},{6,14},{7,15},{8,0},{9,1},... | collective-permute-start | bytes 946184 | tf_op jit(solution)/shard_map/ppermute | solution.py:30
  5.6 0.7 %collective-permute-start.1 = (f32[576,128]{1,0:T(8,128)S(1)}, f32[576,128]{1,0:T(8,128)S(1)}, u32[]{:S(2)}, u32[]{:S(2)}) collective-permute-start(f32[576,128]{1,0:T(8,128)S(1)} %get-tuple-element.23), channel_id=1, source_target_pairs={{0,0},{1,1},{2,2},{3,3},{4,4},{5,5},{6,6},{7,7},{8,16},{9,17},{10,... | collective-permute-start | bytes 884744 | tf_op jit(solution)/shard_map/ppermute | solution.py:30
  6.3 1.6 %collective-permute-start.2 = (f32[328,128]{1,0:T(8,128)S(1)}, f32[328,128]{1,0:T(8,128)S(1)}, u32[]{:S(2)}, u32[]{:S(2)}) collective-permute-start(f32[328,128]{1,0:T(8,128)S(1)} %get-tuple-element.24), channel_id=1, source_target_pairs={{0,1},{1,0},{2,3},{3,2},{4,5},{5,4},{6,7},{7,6},{8,9},{9,8},{10,11... | collective-permute-start | bytes 503816 | tf_op jit(solution)/shard_map/ppermute | solution.py:30
  7.8 4.3 %collective-permute-start.3 = (f32[80,128]{1,0:T(8,128)S(1)}, f32[80,128]{1,0:T(8,128)S(1)}, u32[]{:S(2)}, u32[]{:S(2)}) collective-permute-start(f32[80,128]{1,0:T(8,128)S(1)} %get-tuple-element.25), channel_id=1, source_target_pairs={{0,9},{1,8},{2,11},{3,10},{4,13},{5,12},{6,15},{7,14},{8,1},{9,0},... | collective-permute-start | bytes 122888 | tf_op jit(solution)/shard_map/ppermute | solution.py:30
  12.2 2.9 %collective-permute-done.3.refs_3_ = f32[80,128]{1,0:T(8,128)S(1)} collective-permute-done((f32[80,128]{1,0:T(8,128)S(1)}, f32[80,128]{1,0:T(8,128)S(1)}, u32[]{:S(2)}, u32[]{:S(2)}) %collective-permute-start.3) | collective-permute-done | bytes 40992 | tf_op jit(solution)/shard_map/ppermute | solution.py:30
  15.0 0.0 collective-permute-done.2.refs_2_
  15.0 0.0 collective-permute-done.refs_0_.refs_1_
  15.0 2.7 %collective-permute-start.5 = (f32[160,128]{1,0:T(8,128)S(1)}, f32[160,128]{1,0:T(8,128)S(1)}, u32[]{:S(2)}, u32[]{:S(2)}) collective-permute-start(f32[160,128]{1,0:T(8,128)S(1)} %join.1.refs_0_), channel_id=1, source_target_pairs={{0,16},{1,17},{2,18},{3,19},{4,20},{5,21},{6,22},{7,23},{8,24},{9,... | collective-permute-start | bytes 245768 | tf_op jit(solution)/shard_map/ppermute | solution.py:30
  17.7 0.7 %collective-permute-start.4 = (f32[40,128]{1,0:T(8,128)S(1)}, f32[40,128]{1,0:T(8,128)S(1)}, u32[]{:S(2)}, u32[]{:S(2)}) collective-permute-start(f32[40,128]{1,0:T(8,128)S(1)} %get-tuple-element.26), channel_id=1, source_target_pairs={{0,1},{1,0},{2,3},{3,2},{4,5},{5,4},{6,7},{7,6},{8,17},{9,16},{10,... | collective-permute-start | bytes 61448 | tf_op jit(solution)/shard_map/ppermute | solution.py:30
  18.4 3.1 %collective-permute-done.4.refs_4_ = f32[40,128]{1,0:T(8,128)S(1)} collective-permute-done((f32[40,128]{1,0:T(8,128)S(1)}, f32[40,128]{1,0:T(8,128)S(1)}, u32[]{:S(2)}, u32[]{:S(2)}) %collective-permute-start.4) | collective-permute-done | bytes 20512 | tf_op jit(solution)/shard_map/ppermute | solution.py:30
  21.5 0.0 collective-permute-done.1.refs_1_
  21.5 3.7 %strip.1 = (f32[9,1184,128]{2,1,0:T(8,128)S(1)}, f32[9,2,40,128]{3,2,1,0:T(8,128)S(1)}, f32[3,40,128]{2,1,0:T(8,128)S(1)}, f32[3,40,128]{2,1,0:T(8,128)S(1)}) custom-call(f32[9,512,128]{2,1,0:T(8,128)S(1)} %get-tuple-element.21.own, f32[616,128]{1,0:T(8,128)S(1)} %collective-permute-done.refs_0_.refs_1_, f32[576,128]{1,0:T(8,128)S(1)} %collective-permute-done.1.refs_1_, ...), custom_call_target="tpu_custom_call" | custom-call | tf_op jit(solution)/shard_map/strip/pallas_call | solution.py:507
  25.2 0.0 collective-permute-done.5.refs_1_
  25.2 1.1 %lines.1 = (f32[56,128]{1,0:T(8,128)S(1)}, f32[176,128]{1,0:T(8,128)S(1)}, f32[56,128]{1,0:T(8,128)S(1)}, f32[176,128]{1,0:T(8,128)S(1)}) custom-call(f32[160,128]{1,0:T(8,128)S(1)} %join.1.refs_0_, f32[160,128]{1,0:T(8,128)S(1)} %collective-permute-done.5.refs_1_, f32[3,40,128]{2,1,0:T(8,128)S(1)} %get-tuple-element.30.refs_2_, ...), custom_call_target="tpu_custom_call" | custom-call | tf_op jit(solution)/shard_map/lines/pallas_call | solution.py:525
  26.3 0.1 collective-permute-start.6
  26.4 1.6 %collective-permute-start.8 = (f32[176,128]{1,0:T(8,128)S(1)}, f32[176,128]{1,0:T(8,128)S(1)}, u32[]{:S(2)}, u32[]{:S(2)}) collective-permute-start(f32[176,128]{1,0:T(8,128)S(1)} %get-tuple-element.35), channel_id=1, source_target_pairs={{0,6},{1,7},{2,4},{3,5},{4,2},{5,3},{6,0},{7,1},{8,14},{9,15},{10,... | collective-permute-start | bytes 270344 | tf_op jit(solution)/shard_map/ppermute | solution.py:30
  28.0 0.5 %collective-permute-start.7 = (f32[56,128]{1,0:T(8,128)S(1)}, f32[56,128]{1,0:T(8,128)S(1)}, u32[]{:S(2)}, u32[]{:S(2)}) collective-permute-start(f32[56,128]{1,0:T(8,128)S(1)} %get-tuple-element.34), channel_id=1, source_target_pairs={{0,4},{1,5},{2,6},{3,7},{4,0},{5,1},{6,2},{7,3},{8,12},{9,13},{10,... | collective-permute-start | bytes 86024 | tf_op jit(solution)/shard_map/ppermute | solution.py:30
  28.5 3.5 %collective-permute-done.7.refs_4_ = f32[56,128]{1,0:T(8,128)S(1)} collective-permute-done((f32[56,128]{1,0:T(8,128)S(1)}, f32[56,128]{1,0:T(8,128)S(1)}, u32[]{:S(2)}, u32[]{:S(2)}) %collective-permute-start.7) | collective-permute-done | bytes 28704 | tf_op jit(solution)/shard_map/ppermute | solution.py:30
  32.0 0.0 collective-permute-done.6.refs_3_
  32.0 0.0 collective-permute-done.8.refs_5_
  32.0 8.6 %steps.1 = (f32[3,512,128]{2,1,0:T(8,128)}, f32[512,128]{1,0:T(8,128)}, f32[512,128]{1,0:T(8,128)}) custom-call(f32[9,1184,128]{2,1,0:T(8,128)S(1)} %get-tuple-element.27.refs_0_, f32[9,2,40,128]{3,2,1,0:T(8,128)S(1)} %get-tuple-element.28.refs_1_, f32[56,128]{1,0:T(8,128)S(1)} %get-tuple-element.32.refs_2_, f32[176,128]{1,0:T(8,128)S(1)} %collective-permute-done.6.refs_3_, ...), custom_call_target="tpu_custom_call" | custom-call | tf_op jit(solution)/shard_map/steps/pallas_call | solution.py:549
  (1 shorter events, 0.0 us)
Async XLA Ops:
  2.5 12.5 %collective-permute-start = (f32[616,128]{1,0:T(8,128)S(1)}, f32[616,128]{1,0:T(8,128)S(1)}, u32[]{:S(2)}, u32[]{:S(2)}) collective-permute-start(f32[616,128]{1,0:T(8,128)S(1)} %get-tuple-element.22), channel_id=1, source_target_pairs={{0,8},{1,9},{2,10},{3,11},{4,12},{5,13},{6,14},{7,15},{8,0},{9,1},... | collective-permute-start | bytes 946184 | tf_op jit(solution)/shard_map/ppermute | solution.py:30
  5.6 15.9 %collective-permute-start.1 = (f32[576,128]{1,0:T(8,128)S(1)}, f32[576,128]{1,0:T(8,128)S(1)}, u32[]{:S(2)}, u32[]{:S(2)}) collective-permute-start(f32[576,128]{1,0:T(8,128)S(1)} %get-tuple-element.23), channel_id=1, source_target_pairs={{0,0},{1,1},{2,2},{3,3},{4,4},{5,5},{6,6},{7,7},{8,16},{9,17},{10,... | collective-permute-start | bytes 884744 | tf_op jit(solution)/shard_map/ppermute | solution.py:30
  6.3 8.8 %collective-permute-start.2 = (f32[328,128]{1,0:T(8,128)S(1)}, f32[328,128]{1,0:T(8,128)S(1)}, u32[]{:S(2)}, u32[]{:S(2)}) collective-permute-start(f32[328,128]{1,0:T(8,128)S(1)} %get-tuple-element.24), channel_id=1, source_target_pairs={{0,1},{1,0},{2,3},{3,2},{4,5},{5,4},{6,7},{7,6},{8,9},{9,8},{10,11... | collective-permute-start | bytes 503816 | tf_op jit(solution)/shard_map/ppermute | solution.py:30
  7.8 7.2 %collective-permute-start.3 = (f32[80,128]{1,0:T(8,128)S(1)}, f32[80,128]{1,0:T(8,128)S(1)}, u32[]{:S(2)}, u32[]{:S(2)}) collective-permute-start(f32[80,128]{1,0:T(8,128)S(1)} %get-tuple-element.25), channel_id=1, source_target_pairs={{0,9},{1,8},{2,11},{3,10},{4,13},{5,12},{6,15},{7,14},{8,1},{9,0},... | collective-permute-start | bytes 122888 | tf_op jit(solution)/shard_map/ppermute | solution.py:30
  15.0 10.1 %collective-permute-start.5 = (f32[160,128]{1,0:T(8,128)S(1)}, f32[160,128]{1,0:T(8,128)S(1)}, u32[]{:S(2)}, u32[]{:S(2)}) collective-permute-start(f32[160,128]{1,0:T(8,128)S(1)} %join.1.refs_0_), channel_id=1, source_target_pairs={{0,16},{1,17},{2,18},{3,19},{4,20},{5,21},{6,22},{7,23},{8,24},{9,... | collective-permute-start | bytes 245768 | tf_op jit(solution)/shard_map/ppermute | solution.py:30
  17.7 3.8 %collective-permute-start.4 = (f32[40,128]{1,0:T(8,128)S(1)}, f32[40,128]{1,0:T(8,128)S(1)}, u32[]{:S(2)}, u32[]{:S(2)}) collective-permute-start(f32[40,128]{1,0:T(8,128)S(1)} %get-tuple-element.26), channel_id=1, source_target_pairs={{0,1},{1,0},{2,3},{3,2},{4,5},{5,4},{6,7},{7,6},{8,17},{9,16},{10,... | collective-permute-start | bytes 61448 | tf_op jit(solution)/shard_map/ppermute | solution.py:30
  26.3 5.7 %collective-permute-start.6 = (f32[176,128]{1,0:T(8,128)S(1)}, f32[176,128]{1,0:T(8,128)S(1)}, u32[]{:S(2)}, u32[]{:S(2)}) collective-permute-start(f32[176,128]{1,0:T(8,128)S(1)} %get-tuple-element.33), channel_id=1, source_target_pairs={{0,2},{1,3},{2,0},{3,1},{4,6},{5,7},{6,4},{7,5},{8,10},{9,11},{10,... | collective-permute-start | bytes 270344 | tf_op jit(solution)/shard_map/ppermute | solution.py:30
  26.4 5.6 %collective-permute-start.8 = (f32[176,128]{1,0:T(8,128)S(1)}, f32[176,128]{1,0:T(8,128)S(1)}, u32[]{:S(2)}, u32[]{:S(2)}) collective-permute-start(f32[176,128]{1,0:T(8,128)S(1)} %get-tuple-element.35), channel_id=1, source_target_pairs={{0,6},{1,7},{2,4},{3,5},{4,2},{5,3},{6,0},{7,1},{8,14},{9,15},{10,... | collective-permute-start | bytes 270344 | tf_op jit(solution)/shard_map/ppermute | solution.py:30
  28.0 4.0 %collective-permute-start.7 = (f32[56,128]{1,0:T(8,128)S(1)}, f32[56,128]{1,0:T(8,128)S(1)}, u32[]{:S(2)}, u32[]{:S(2)}) collective-permute-start(f32[56,128]{1,0:T(8,128)S(1)} %get-tuple-element.34), channel_id=1, source_target_pairs={{0,4},{1,5},{2,6},{3,7},{4,0},{5,1},{6,2},{7,3},{8,12},{9,13},{10,... | collective-permute-start | bytes 86024 | tf_op jit(solution)/shard_map/ppermute | solution.py:30

commit v2 on v1

--- a/solution.py
+++ b/solution.py
@@ -102,9 +102,9 @@
                 zb[pl.ds((f * W + l) * cx, cx), :] = jnp.where(ez, low, high)
 
 
-def join_kernel(*refs):
-    *ins, out = refs
-    rows = out.shape[0] // len(ins)
+def join_kernel(*refs, count):
+    ins, out = refs[:count], refs[-1]
+    rows = out.shape[0] // count
     for i, ref in enumerate(ins):
         out[i * rows:(i + 1) * rows, :] = ref[ref.shape[0] - rows:, :]
 
@@ -156,15 +156,29 @@
     return pltpu.roll(value, by % size, axis)
 
 
-def add_strips(low, high, row, x, cy):
+def add_strips(low, high, row, x, cy, bounded=False):
     at = COLS * (x + W)
     lane = lane_of(row.shape)
-    low = jnp.where(lane >= at + W, roll(row, at + W, 1), low)
-    high = jnp.where(lane >= at, roll(row, at - (cy - 2 * W), 1), high)
+    here, there = lane >= at + W, lane >= at
+    if bounded:
+        here, there = here & (lane < at + COLS), there & (lane < at + 2 * W)
+    low = jnp.where(here, roll(row, at + W, 1), low)
+    high = jnp.where(there, roll(row, at - (cy - 2 * W), 1), high)
     return low, high
 
 
-def strip_kernel(fields, xa, xb, za, zb, xza, xzb, xzc, xzd, ext, strips, ya, yb, depths, edges, *, dims, counts):
+def own_kernel(fields, strips, *, dims):
+    cz, cx, cy = dims
+    for f in range(FIELDS):
+        low = jnp.zeros((cz, cy), jnp.float32)
+        high = jnp.zeros((cz, cy), jnp.float32)
+        for x in range(cx):
+            low, high = add_strips(low, high, fields[f, pl.ds(x, cz, stride=cx), :], x, cy)
+        strips[f, 0] = low
+        strips[f, 1] = high
+
+
+def halo_kernel(fields, mine, xa, xb, za, zb, xza, xzb, xzc, xzd, ext, strips, ya, yb, depths, edges, *, dims, counts):
     cz, cx, cy = dims
     _, wide, _ = rows_of(dims)
     planes = cz + 8
@@ -173,29 +187,31 @@
     ey = even(place[1][0])
     lane = lane_of((planes, cy))
     middle = (lane % COLS >= W) & (lane % COLS < 2 * W)
+    halo = list(range(-W, 0)) + list(range(cx, cx + W))
     for g in range(FIELDS // 3):
         outs = [jnp.zeros((planes, cy), jnp.float32)] * 2
         for j in range(3):
             f = 3 * g + j
-            low = jnp.zeros((planes, cy), jnp.float32)
-            high = jnp.zeros((planes, cy), jnp.float32)
+            low, high = mine[f, 0], mine[f, 1]
+            for x in halo:
+                row = ext[f, pl.ds(W * wide + BASE + x, cz, stride=wide), :]
+                low, high = add_strips(low, high, row, x, cy, True)
+            below = jnp.zeros((8, cy), jnp.float32)
+            above = jnp.zeros((8, cy), jnp.float32)
             for x in range(-W, cx + W):
-                own = ext[f, pl.ds(W * wide + BASE + x, cz, stride=wide), :]
-                if 0 <= x < cx:
-                    beyond = depths[f, pl.ds(x, 8, stride=cx), :]
-                else:
-                    beyond = edges[f, x + W if x < 0 else x - cx + W]
-                low, high = add_strips(low, high, jnp.concatenate([own, beyond]), x, cy)
+                row = depths[f, pl.ds(x, 8, stride=cx), :] if 0 <= x < cx else edges[f, x + W if x < 0 else x - cx + W]
+                below, above = add_strips(below, above, row, x, cy)
+            low, high = jnp.concatenate([low, below]), jnp.concatenate([high, above])
             strips[f, 0] = low
             strips[f, 1] = high
             for n, (odd_side, even_side) in enumerate(((low, high), (high, low))):
-                mine = jnp.where(middle, jnp.where(ey, even_side, odd_side), 0.0)
-                outs[n] = outs[n] + roll(mine, W * (j - 1), 1)
+                edge = jnp.where(middle, jnp.where(ey, even_side, odd_side), 0.0)
+                outs[n] = outs[n] + roll(edge, W * (j - 1), 1)
         ya[g] = outs[0]
         yb[g] = outs[1]
 
 
-def lines_kernel(own_rows, far_rows, ya, yb, *refs, dims, counts, rows, joined):
+def lines_kernel(own_rows, far_rows, ya, yb, before, *refs, dims, counts, rows, joined):
     _, cx, cy = dims
     nx, ny, _ = counts
     _, _, wide = rows_of(dims)
@@ -275,40 +291,38 @@
     return av + [m, shear]
 
 
-def main_steps(ext, forced_z, force, outs, scratch, dims, place):
+def lap(below, a, above, lower, upper):
+    return (above + below) + (lower + upper) + (roll(a, 1, 1) + roll(a, -1, 1)) - 6.0 * a
+
+
+def first_kernel(ext, b0, v1, a1, w1, m0, w0, *, dims, counts):
     cz, cx, cy = dims
     _, wide, short = rows_of(dims)
-    (ix, nx), _, (iz, nz) = place
-    out_v, out_p, out_s = outs
-    w0, b0, v1, a1, w1, q1 = scratch
+    (ix, nx), _, (iz, nz) = [(lax.axis_index(a), n) for a, n in zip(AXES, counts)]
 
     row = lax.broadcasted_iota(jnp.int32, (short, cy), 0)
     inside1 = ((row > 0) & (row <= cx)) | ((row > cx) & (ix < nx - 1)) | ((row == 0) & (ix > 0))
-    inside0 = (row < cx) | (ix < nx - 1)
-
-    def keep(a, inside, plane):
+
+    def keep(a, plane):
         at = iz * cz + plane - W
-        return jnp.where(inside & ((at >= 0) & (at < nz * cz)), a, 0.0)
-
-    def lap(below, a, above, lower, upper):
-        return (above + below) + (lower + upper) + (roll(a, 1, 1) + roll(a, -1, 1)) - 6.0 * a
+        return jnp.where(inside1 & ((at >= 0) & (at < nz * cz)), a, 0.0)
 
     def wider(f, plane, dx=0):
-        at = pl.ds(plane * wide + (BASE - 1 + dx), short)
-        return forced_z[at, :] if f == 7 else ext[f, at, :]
+        return ext[f, pl.ds(plane * wide + (BASE - 1 + dx), short), :]
 
     def weight(c, plane, dx=0):
         return w0[c, pl.ds(plane * wide + (BASE - 1 + dx), short), :]
 
-    def weigh(plane):
+    def weigh(plane, _):
         at = pl.ds(pl.multiple_of(plane * wide, 8), wide)
         for c in range(3):
-            w0[c, at, :] = ext[4, at, :] * (forced_z[at, :] if c == 2 else ext[5 + c, at, :])
+            w0[c, at, :] = ext[4, at, :] * ext[5 + c, at, :]
+        return 0
 
     def pressure(plane, base, q, scale):
         vx, vy, vz = (wider(base + c, plane) for c in range(3))
         d = (vx - wider(base, plane, -1)) + (vy - roll(vy, 1, 1)) + (vz - wider(base + 2, plane - 1))
-        return keep(wider(q, plane) + scale * d, inside1, plane)
+        return keep(wider(q, plane) + scale * d, plane)
 
     def whole(plane):
         return pl.ds(pl.multiple_of(plane * short, 8), short)
@@ -317,33 +331,39 @@
         p1, m = carry
         p1_above = pressure(plane + 1, 0, 3, 1.0)
         m_above = pressure(plane + 1, 5, 8, -0.25)
-        q1[0, whole(plane + 1), :] = p1_above
-        q1[1, whole(plane + 1), :] = m_above
-        next_row = pl.ds(plane * short + 1, short)
-        g = (q1[0, next_row, :] - p1, roll(p1, -1, 1) - p1, p1_above - p1)
-        h = (q1[1, next_row, :] - m, roll(m, -1, 1) - m, m_above - m)
+        m0[whole(plane + 1), :] = m_above
+        g = (roll(p1, -1, 0) - p1, roll(p1, -1, 1) - p1, p1_above - p1)
+        h = (roll(m, -1, 0) - m, roll(m, -1, 1) - m, m_above - m)
         mod = wider(4, plane)
-        weigh(plane + 2)
         for c in range(3):
             v = wider(c, plane)
             bend = lap(wider(c, plane - 1), v, wider(c, plane + 1), wider(c, plane, -1), wider(c, plane, 1))
             b0[c, whole(plane), :] = bend
-            v1[c, whole(plane), :] = keep(v + 0.25 * (g[c] + mod * bend), inside1, plane)
+            v1[c, whole(plane), :] = keep(v + 0.25 * (g[c] + mod * bend), plane)
             a = wider(5 + c, plane)
             spring = lap(weight(c, plane - 1), weight(c, plane), weight(c, plane + 1), weight(c, plane, -1), weight(c, plane, 1))
-            a = keep(a + 0.25 * spring - h[c], inside1, plane)
-            if c == 2:
-                a = a + jnp.where(plane == W, force[pl.ds(1, short), :], 0.0)
+            a = keep(a + 0.25 * spring - h[c], plane)
             a1[c, whole(plane), :] = a
             w1[c, whole(plane), :] = mod * a
         return p1_above, m_above
 
-    for plane in range(3):
-        weigh(plane)
+    lax.fori_loop(0, cz + 2 * W, weigh, 0, unroll=4)
     begin = (pressure(1, 0, 3, 1.0), pressure(1, 5, 8, -0.25))
-    for i in range(2):
-        q1[i, whole(1), :] = begin[i]
+    m0[whole(1), :] = begin[1]
     lax.fori_loop(1, cz + W + 1, first, begin, unroll=2)
+
+
+def second_kernel(ext, b0, v1, a1, w1, m0, out_v, out_p, out_s, bends, *, dims, counts):
+    cz, cx, cy = dims
+    _, wide, short = rows_of(dims)
+    (ix, nx), _, (iz, nz) = [(lax.axis_index(a), n) for a, n in zip(AXES, counts)]
+
+    row = lax.broadcasted_iota(jnp.int32, (short, cy), 0)
+    inside0 = (row < cx) | (ix < nx - 1)
+
+    def keep(a, plane):
+        at = iz * cz + plane - W
+        return jnp.where(inside0 & ((at >= 0) & (at < nz * cz)), a, 0.0)
 
     def step(ref, c, plane, dx=0, count=cx):
         return ref[c, pl.ds(plane * short + (1 + dx), count), :]
@@ -351,13 +371,13 @@
     def pressure1(plane):
         ax, ay, az = (step(a1, c, plane, 0, short) for c in range(3))
         d = (ax - step(a1, 0, plane, -1, short)) + (ay - roll(ay, 1, 1)) + (az - step(a1, 2, plane - 1, 0, short))
-        return keep(step(q1, 1, plane, 0, short) - 0.25 * d, inside0, plane)
+        return keep(m0[pl.ds(plane * short + 1, short), :] - 0.25 * d, plane)
 
     def second(plane, m):
         m_above = pressure1(plane + 1)
-        q1[2, whole(plane + 1), :] = m_above
+        upper = roll(m, -1, 0)[:cx]
         m, above = m[:cx], m_above[:cx]
-        h = (q1[2, pl.ds(plane * short + 1, cx), :] - m, roll(m, -1, 1) - m, above - m)
+        h = (upper - m, roll(m, -1, 1) - m, above - m)
         own = pl.ds(pl.multiple_of((plane - W) * cx, 8), cx)
         shear = jnp.zeros((cx, cy), jnp.float32)
         for c in range(3):
@@ -370,25 +390,77 @@
                 step(w1, c, plane - 1), step(w1, c, plane), step(w1, c, plane + 1), step(w1, c, plane, -1),
                 step(w1, c, plane, 1),
             )
-            at = pl.ds(pl.multiple_of(plane * wide + BASE, 8), cx)
-            at_first = forced_z[at, :] if c == 2 else ext[5 + c, at, :]
+            at_first = ext[5 + c, pl.ds(pl.multiple_of(plane * wide + BASE, 8), cx), :]
             shear = shear + (at_first * bend + a * step(b0, c, plane))
             out_v[c, own, :] = a + 0.25 * spring - h[c]
         out_p[own, :] = m
         out_s[own, :] = 0.25 * shear
         return m_above
 
-    begin = pressure1(W)
-    q1[2, whole(W), :] = begin
-    lax.fori_loop(W, cz + W, second, begin, unroll=2)
-
-
-def steps_kernel(ext, strips, *rest, dims, counts, lines, joined):
+    lax.fori_loop(W, cz + W, second, pressure1(W), unroll=2)
+    for c in range(3):
+        for k in range(2):
+            bends[3 * k + c] = step(b0, c, W + k)
+    bends[6] = lap(
+        step(v1, 2, W - 1), step(v1, 2, W), step(v1, 2, W + 1), step(v1, 2, W, -1), step(v1, 2, W, 1)
+    )
+
+
+def forcing_steps(force, ext, bends, dims, place):
+    cz, cx, cy = dims
+    _, wide, short = rows_of(dims)
+    ix, nx = place[0]
+    f0, f1 = force[0:short, :], force[pl.ds(short, short), :]
+    mod = [ext[4, pl.ds((W + z) * wide + BASE - W, short), :] for z in range(2)]
+    x = lax.broadcasted_iota(jnp.int32, (short, cy), 0) - W
+    inside = ((x >= 0) & (x < cx)) | ((x >= cx) & (ix < nx - 1)) | ((x < 0) & (ix > 0))
+
+    def keep(a):
+        return jnp.where(inside, a, 0.0)
+
+    def flat(a):
+        return roll(a, 1, 0) + roll(a, -1, 0) + roll(a, 1, 1) + roll(a, -1, 1) - 6.0 * a
+
+    def grad(q):
+        return [roll(q, -1, 0) - q, roll(q, -1, 1) - q]
+
+    w = mod[0] * f1
+    m = [-0.25 * f1, 0.25 * f1]
+    g = [grad(q) for q in m]
+    a = [
+        [keep(-g[0][0]), keep(-g[0][1]), keep(f1 + 0.25 * flat(w) - (m[1] - m[0])) + f0],
+        [keep(-g[1][0]), keep(-g[1][1]), keep(0.25 * w + m[1])],
+    ]
+    w = [[mod[z] * a[z][c] for c in range(3)] for z in range(2)]
+
+    def div(u):
+        return (u[0] - roll(u[0], 1, 0)) + (u[1] - roll(u[1], 1, 1)) + u[2]
+
+    m = [keep(m[0] - 0.25 * div(a[0])), keep(m[1] - 0.25 * (div(a[1]) - a[0][2])), keep(0.25 * a[1][2])]
+    g = [grad(q) for q in m]
+    deep = [m[1] - m[0], m[2] - m[1], -m[2]]
+    own = slice(W, W + cx)
+    out = []
+    for z in range(3):
+        add = []
+        for c in range(3):
+            spring = (flat(w[z][c]) + w[1 - z][c]) if z < 2 else w[1][c]
+            start = a[z][c] if z < 2 else 0.0
+            add.append((start + 0.25 * spring - (g[z][c] if c < 2 else deep[z]))[own])
+        add.append(m[z][own])
+        if z < 2:
+            meet = sum(a[z][c][own] * bends[3 * z + c] for c in range(3))
+            add.append(0.25 * (meet + f1[own] * bends[6] if z == 0 else meet))
+        out.append(add)
+    return out
+
+
+def finish_kernel(ext, strips, main_v, main_p, main_s, bends, *rest, dims, counts, lines, joined):
     cz, cx, cy = dims
     _, wide, short = rows_of(dims)
     planes = cz + 8
     forced = rest[:lines]
-    out_v, out_p, out_s, force, forced_z, *scratch = rest[lines:]
+    out_v, out_p, out_s, force, stage, sem = rest[lines:]
     place = [(lax.axis_index(a), n) for a, n in zip(AXES, counts)]
     (ix, nx), (iy, ny), (iz, nz) = place
     block = STEPS * short
@@ -397,10 +469,6 @@
     for ref in forced[1:]:
         total = total + ref[ref.shape[0] - size:, :]
     force[...] = jnp.where(iz == 0, total, 0.0)
-    surface = pl.ds(W * wide + BASE - W, short)
-    forced_z[...] = ext[7]
-    forced_z[surface, :] = forced_z[surface, :] + force[pl.ds(short, short), :]
-    main_steps(ext, forced_z, force, (out_v, out_p, out_s), scratch, dims, place)
 
     lane = lane_of((planes, cy))
     depth = lax.broadcasted_iota(jnp.int32, (planes, cy), 0)
@@ -426,16 +494,28 @@
         top = depth == 0
         push = [jnp.where(top, force[pl.ds(block + 2 * t + side, 1), :], 0.0) for t in range(STEPS)]
         results.append(strip_steps(s, solid & beyond, push[1], push[0]))
+    added = forcing_steps(force, ext, bends, dims, place)
+    mains = [main_v.at[0], main_v.at[1], main_v.at[2], main_p, main_s]
     outs = [out_v.at[0], out_v.at[1], out_v.at[2], out_p, out_s]
     lane = lane_of((cz, cy))
-    for low, high, ref in zip(*results, outs):
+    copies = []
+    for n, (low, high, main, out) in enumerate(zip(*results, mains, outs)):
+        reach = [add[n] for add in added if n < len(add)]
+        done = len(reach) * cx
+        stage[n, 0:done, :] = main[0:done, :] + jnp.concatenate(reach)
+        stage[n, done:, :] = main[done:, :]
         low, high = low[:cz], high[:cz]
         for x0 in range(cx):
             start = COLS * (x0 + W)
-            value = ref[pl.ds(x0, cz, stride=cx), :]
+            value = stage[n, pl.ds(x0, cz, stride=cx), :]
             value = jnp.where(lane < W, roll(low, -(start + W), 1), value)
             value = jnp.where(lane >= cy - W, roll(high, cy - W - (start + W), 1), value)
-            ref[pl.ds(x0, cz, stride=cx), :] = value
+            stage[n, pl.ds(x0, cz, stride=cx), :] = value
+        copy = pltpu.make_async_copy(stage.at[n], out, sem.at[n])
+        copy.start()
+        copies.append(copy)
+    for copy in copies:
+        copy.wait()
 
 
 def shards(vel, pres, modulus, adj_vel_in, adj_pres_in, sensor_values, sensor_owner, sensor_line, sensor_step):
@@ -479,17 +559,25 @@
 
     def halo(value, sx, sz):
         def partner(i, j, k):
-            return i if sx is None else mate(i, nx, sx), j, k if sz is None else mate(k, nz, sz)
+            a, c = i if sx is None else mate(i, nx, sx), k if sz is None else mate(k, nz, sz)
+            return (a, j, c) if (a, c) != (i, k) else (a, mate(j, ny, 0), c)
 
         return exchange(value, counts, partner)
 
     halos = spread_out([halo(value, *seconds[i]) for i, value in zip(spots, packed)])
 
+    mine = pl.pallas_call(
+        functools.partial(own_kernel, dims=dims), out_shape=struct(FIELDS, 2, cz, cy), in_specs=[VM], out_specs=VM,
+        compiler_params=PARAMS, name="own",
+        cost_estimate=pl.CostEstimate(flops=20_000_000, bytes_accessed=4_000_000, transcendentals=0),
+    )(fields)
+
     parts = [sens, halos[0]] if deep else [sens, halos[0], halos[2], halos[4]]
+    rest = [x for x in halos if x is not None and not any(x is p for p in parts)] + [mine]
     near = pl.pallas_call(
-        join_kernel, out_shape=struct(len(parts) * size, cy), in_specs=[VM] * len(parts), out_specs=VM,
-        compiler_params=PARAMS, name="join",
-    )(*parts)
+        functools.partial(join_kernel, count=len(parts)), out_shape=struct(len(parts) * size, cy),
+        in_specs=[VM] * len(parts + rest), out_specs=VM, compiler_params=PARAMS, name="join",
+    )(*parts, *rest)
     far, reach = None, 2
     while reach < nx:
         if far is not None:
@@ -500,16 +588,24 @@
     depth = cz + 8
     y_face = struct(FIELDS // 3, depth, cy)
 
-    def strip(own, *refs):
+    def halo_fill(own, strips, *refs):
         count = len(spots)
-        strip_kernel(own, *spread_out(refs[:count]), *refs[count:], dims=dims, counts=counts)
+        halo_kernel(own, strips, *spread_out(refs[:count]), *refs[count:], dims=dims, counts=counts)
 
     ext, strips, ya, yb = pl.pallas_call(
-        strip, out_shape=[pltpu.VMEM((FIELDS, planes * wide, cy), jnp.float32), struct(FIELDS, 2, depth, cy), y_face, y_face],
-        in_specs=[VM] * (1 + len(spots)), out_specs=[VM] * 4,
+        halo_fill, out_shape=[pltpu.VMEM((FIELDS, planes * wide, cy), jnp.float32), struct(FIELDS, 2, depth, cy), y_face, y_face],
+        in_specs=[VM] * (2 + len(spots)), out_specs=[VM] * 4,
         scratch_shapes=[pltpu.VMEM((FIELDS, 8 * cx, cy), jnp.float32), pltpu.VMEM((FIELDS, 2 * W, 8, cy), jnp.float32)],
-        compiler_params=PARAMS, name="strip",
-    )(fields, *[halos[i] for i in spots])
+        compiler_params=PARAMS, name="halo",
+    )(fields, mine, *[halos[i] for i in spots])
+
+    three = pltpu.VMEM((3, planes * short + 8, cy), jnp.float32)
+    middle = pl.pallas_call(
+        functools.partial(first_kernel, dims=dims, counts=counts), out_shape=[three] * 4 + [pltpu.VMEM(three.shape[1:], jnp.float32)],
+        in_specs=[VM], out_specs=[VM] * 5, scratch_shapes=[pltpu.VMEM((3, planes * wide, cy), jnp.float32)],
+        compiler_params=PARAMS, name="first",
+        cost_estimate=pl.CostEstimate(flops=30_000_000, bytes_accessed=10_000_000, transcendentals=0),
+    )(ext)
 
     second = ny - 1 if ny == 4 else ny
     joined = (1, second)
@@ -524,9 +620,9 @@
     gathered = [near] if far is None else [near, far]
     forced = pl.pallas_call(
         lines, out_shape=[struct(line_rows + (strip_rows if k in joined else 0), cy) for k in range(ny)],
-        in_specs=[VM] * (len(gathered) + 2), out_specs=[VM] * ny,
+        in_specs=[VM] * (len(gathered) + 3), out_specs=[VM] * ny,
         scratch_shapes=[pltpu.VMEM((ny + 2, STEPS * short, cy), jnp.float32)], compiler_params=PARAMS, name="lines",
-    )(*gathered, ya, yb)
+    )(*gathered, ya, yb, middle[-1])
     forced = [forced[0]] + [exchange(forced[k], counts, lambda i, j, m, k=k: (i, j ^ k, m)) for k in range(1, ny)]
     if second == ny:
         yb = exchange(yb, counts, lambda i, j, k: (i, mate(j, ny, 1), k))
@@ -541,20 +637,26 @@
         joined = (1, len(forced))
         forced.append(jnp.concatenate([yb.reshape(strip_rows, cy), jnp.zeros((line_rows, cy), jnp.float32)]))
 
-    def steps(*refs):
-        steps_kernel(*refs, dims=dims, counts=counts, lines=len(forced), joined=joined)
-
-    three = pltpu.VMEM((3, planes * short + 8, cy), jnp.float32)
-    whole = pltpu.VMEM((planes * wide, cy), jnp.float32)
+    one, triple = (cz * cx, cy), (3, cz * cx, cy)
+    mains = pl.pallas_call(
+        functools.partial(second_kernel, dims=dims, counts=counts),
+        out_shape=[pltpu.VMEM(triple, jnp.float32), pltpu.VMEM(one, jnp.float32), pltpu.VMEM(one, jnp.float32), struct(7, cx, cy)],
+        in_specs=[VM] * 6, out_specs=[VM] * 4,
+        compiler_params=PARAMS, name="second",
+        cost_estimate=pl.CostEstimate(flops=30_000_000, bytes_accessed=10_000_000, transcendentals=0),
+    )(ext, *middle)
+
+    def finish(*refs):
+        finish_kernel(*refs, dims=dims, counts=counts, lines=len(forced), joined=joined)
+
     out_v, out_p, out_s = pl.pallas_call(
-        steps, out_shape=[struct(3, cz * cx, cy), struct(cz * cx, cy), struct(cz * cx, cy)],
-        in_specs=[VM] * (2 + len(forced)), out_specs=[VM] * 3,
+        finish, out_shape=[struct(*triple), struct(*one), struct(*one)],
+        in_specs=[VM] * (6 + len(forced)), out_specs=[HBM] * 3,
         scratch_shapes=[
-            pltpu.VMEM((line_rows, cy), jnp.float32), whole, pltpu.VMEM((3, planes * wide, cy), jnp.float32),
-            three, three, three, three, three,
+            pltpu.VMEM((line_rows, cy), jnp.float32), pltpu.VMEM((5,) + one, jnp.float32), pltpu.SemaphoreType.DMA((5,)),
         ],
-        compiler_params=PARAMS, name="steps",
-    )(ext, strips, *forced)
+        compiler_params=PARAMS, name="finish",
+    )(ext, strips, *mains, *forced)
     return out_v.reshape(3, cz, cx, cy), out_p.reshape(cz, cx, cy), out_s.reshape(cz, cx, cy)
 
 

time: 40.8 us -> 33.1 us (0.81)
  waiting for transfers between devices: 9.44 us -> 2.89 us
  starting transfers between devices: 15.2 us -> 14.5 us
    ppermute x9, waiting for transfers between devices: 9.44 us -> 2.89 us  [exchange(): return lax.ppermute(value, AXES, pairs)]
    ppermute x9, starting transfers between devices: 15.2 us -> 14.5 us  [exchange(): return lax.ppermute(value, AXES, pairs)]
    pallas_call x3 -> x6, Pallas kernels: 12.3 us -> 11.9 us  [the longest x1 3.4 us: shards(): pl.pallas_call(functools.partial(first_kernel, dims=dims, counts=counts),...]
  transfers between devices with their start and end apart: 9 -> 9, of which waited for: 3 -> 3; matrix products, arithmetic and copies ran while one was open for 0% -> 0% of each run, Pallas kernels for 9% -> 27%
where the time goes in v2:
time: 33.1 us; the launch traced here: 33 us
  Pallas kernels  14.9 us (45%)
  starting transfers between devices  14.5 us (44%)
  waiting for transfers between devices  2.89 us (9%)
  between operations  0.7 us (2%)
    ppermute x9, starting transfers between devices, exchange(): return lax.ppermute(value, AXES, pairs)  14.5 us
    pallas_call x1, Pallas kernels, shards(): pl.pallas_call(functools.partial(first_kernel, dims=dims, counts=counts),...  3.4 us
    pallas_call x1, Pallas kernels, shards(): pl.pallas_call(finish, out_shape=[struct(*triple), struct(*one), struct(*...  2.99 us
    ppermute x9, waiting for transfers between devices, exchange(): return lax.ppermute(value, AXES, pairs)  2.89 us
    pallas_call x1, Pallas kernels, shards(): pl.pallas_call(functools.partial(second_kernel, dims=dims, counts=counts)...  2.51 us
    pallas_call x1, Pallas kernels, shards(): pl.pallas_call(pack, out_shape=[pltpu.VMEM((FIELDS, cz * cx, cy), jnp.flo...  1.86 us
    pallas_call x1, Pallas kernels, shards(): pl.pallas_call(halo_fill, out_shape=[pltpu.VMEM((FIELDS, planes * wide, c...  1.61 us
    pallas_call x1, Pallas kernels, shards(): pl.pallas_call(functools.partial(own_kernel, dims=dims), out_shape=struct...  1.37 us
  transfers between devices with their start and end apart: 9, of which 3 were waited for; matrix products, arithmetic and copies ran while one was open for 0% of the time, Pallas kernels for 27%

profile of v2, /device:TPU:0, one launch (start us, length us, event | category | flops | bytes accessed | tf_op | source)
XLA Modules:
  0.0 33.0 jit_solution(8949892288121789443)
XLA Ops:
  0.6 1.9 %pack.1 = (f32[9,512,128]{2,1,0:T(8,128)S(1)}, f32[616,128]{1,0:T(8,128)S(1)}, f32[576,128]{1,0:T(8,128)S(1)}, f32[328,128]{1,0:T(8,128)S(1)}, f32[80,128]{1,0:T...) custom-call(f32[3,512,128]{2,1,0:T(8,128)} %bitcast.11, f32[512,128]{1,0:T(8,128)} %bitcast.13, ...), custom_call_target="tpu_custom_call" | custom-call | tf_op jit(solution)/shard_map/pack/pallas_call | solution.py:552
  2.5 3.1 %collective-permute-start = (f32[616,128]{1,0:T(8,128)S(1)}, f32[616,128]{1,0:T(8,128)S(1)}, u32[]{:S(2)}, u32[]{:S(2)}) collective-permute-start(f32[616,128]{1,0:T(8,128)S(1)} %get-tuple-element.31), channel_id=1, source_target_pairs={{0,8},{1,9},{2,10},{3,11},{4,12},{5,13},{6,14},{7,15},{8,0},{9,1},... | collective-permute-start | bytes 946184 | tf_op jit(solution)/shard_map/ppermute | solution.py:30
  5.6 0.0 collective-permute-start.1
  5.6 1.5 %collective-permute-start.2 = (f32[328,128]{1,0:T(8,128)S(1)}, f32[328,128]{1,0:T(8,128)S(1)}, u32[]{:S(2)}, u32[]{:S(2)}) collective-permute-start(f32[328,128]{1,0:T(8,128)S(1)} %get-tuple-element.33), channel_id=1, source_target_pairs={{0,1},{1,0},{2,3},{3,2},{4,5},{5,4},{6,7},{7,6},{8,9},{9,8},{10,11... | collective-permute-start | bytes 503816 | tf_op jit(solution)/shard_map/ppermute | solution.py:30
  7.1 3.1 %collective-permute-start.3 = (f32[80,128]{1,0:T(8,128)S(1)}, f32[80,128]{1,0:T(8,128)S(1)}, u32[]{:S(2)}, u32[]{:S(2)}) collective-permute-start(f32[80,128]{1,0:T(8,128)S(1)} %get-tuple-element.34), channel_id=1, source_target_pairs={{0,9},{1,8},{2,11},{3,10},{4,13},{5,12},{6,15},{7,14},{8,1},{9,0},... | collective-permute-start | bytes 122888 | tf_op jit(solution)/shard_map/ppermute | solution.py:30
  10.2 1.5 %collective-permute-start.4 = (f32[40,128]{1,0:T(8,128)S(1)}, f32[40,128]{1,0:T(8,128)S(1)}, u32[]{:S(2)}, u32[]{:S(2)}) collective-permute-start(f32[40,128]{1,0:T(8,128)S(1)} %get-tuple-element.35), channel_id=1, source_target_pairs={{0,1},{1,0},{2,3},{3,2},{4,5},{5,4},{6,7},{7,6},{8,17},{9,16},{10,... | collective-permute-start | bytes 61448 | tf_op jit(solution)/shard_map/ppermute | solution.py:30
  11.7 1.4 %own.1.strips.refs_6_ = f32[9,2,32,128]{3,2,1,0:T(8,128)S(1)} custom-call(f32[9,512,128]{2,1,0:T(8,128)S(1)} %get-tuple-element.30.fields.own), custom_call_target="tpu_custom_call" | custom-call | flops 20000000 | bytes 4000000 | tf_op jit(solution)/shard_map/own/pallas_call | solution.py:569
  13.1 0.9 %collective-permute-done.4.refs_4_.refs_5_ = f32[40,128]{1,0:T(8,128)S(1)} collective-permute-done((f32[40,128]{1,0:T(8,128)S(1)}, f32[40,128]{1,0:T(8,128)S(1)}, u32[]{:S(2)}, u32[]{:S(2)}) %collective-permute-start.4) | collective-permute-done | bytes 20512 | tf_op jit(solution)/shard_map/ppermute | solution.py:30
  14.0 1.0 %collective-permute-done.3.refs_3_ = f32[80,128]{1,0:T(8,128)S(1)} collective-permute-done((f32[80,128]{1,0:T(8,128)S(1)}, f32[80,128]{1,0:T(8,128)S(1)}, u32[]{:S(2)}, u32[]{:S(2)}) %collective-permute-start.3) | collective-permute-done | bytes 40992 | tf_op jit(solution)/shard_map/ppermute | solution.py:30
  15.0 0.0 collective-permute-done.2.refs_2_
  15.0 0.0 collective-permute-done.1.refs_1_.refs_4_
  15.0 0.0 collective-permute-done.refs_0_.refs_1_
  15.1 3.1 %collective-permute-start.5 = (f32[160,128]{1,0:T(8,128)S(1)}, f32[160,128]{1,0:T(8,128)S(1)}, u32[]{:S(2)}, u32[]{:S(2)}) collective-permute-start(f32[160,128]{1,0:T(8,128)S(1)} %join.1.refs_0_), channel_id=1, source_target_pairs={{0,16},{1,17},{2,18},{3,19},{4,20},{5,21},{6,22},{7,23},{8,24},{9,... | collective-permute-start | bytes 245768 | tf_op jit(solution)/shard_map/ppermute | solution.py:30
  18.1 1.6 %halo.1 = (f32[9,1184,128]{2,1,0:T(8,128)S(1)}, f32[9,2,40,128]{3,2,1,0:T(8,128)S(1)}, f32[3,40,128]{2,1,0:T(8,128)S(1)}, f32[3,40,128]{2,1,0:T(8,128)S(1)}) custom-call(f32[9,512,128]{2,1,0:T(8,128)S(1)} %get-tuple-element.30.fields.own, f32[9,2,32,128]{3,2,1,0:T(8,128)S(1)} %own.1.strips.refs_6_, f32[616,128]{1,0:T(8,128)S(1)} %collective-permute-done.refs_0_.refs_1_, ...), custom_call_target="tpu_custom_call" | custom-call | tf_op jit(solution)/shard_map/halo/pallas_call | solution.py:595
  19.8 3.4 %first.1 = (f32[3,896,128]{2,1,0:T(8,128)S(1)}, f32[3,896,128]{2,1,0:T(8,128)S(1)}, f32[3,896,128]{2,1,0:T(8,128)S(1)}, f32[3,896,128]{2,1,0:T(8,128)S(1)}, f32[896,128]{1,0:T(8,128)S(1)}) custom-call(f32[9,1184,128]{2,1,0:T(8,128)S(1)} %get-tuple-element.36.ext.refs_0_), custom_call_target="tpu_custom_call" | custom-call | flops 30000000 | bytes 10000000 | tf_op jit(solution)/shard_map/first/pallas_call | solution.py:603
  23.2 0.0 collective-permute-done.5.refs_1_
  23.2 1.1 %lines.1 = (f32[56,128]{1,0:T(8,128)S(1)}, f32[176,128]{1,0:T(8,128)S(1)}, f32[56,128]{1,0:T(8,128)S(1)}, f32[176,128]{1,0:T(8,128)S(1)}) custom-call(f32[160,128]{1,0:T(8,128)S(1)} %join.1.refs_0_, f32[160,128]{1,0:T(8,128)S(1)} %collective-permute-done.5.refs_1_, f32[3,40,128]{2,1,0:T(8,128)S(1)} %get-tuple-element.48.refs_2_, ...), custom_call_target="tpu_custom_call" | custom-call | tf_op jit(solution)/shard_map/lines/pallas_call | solution.py:621
  24.3 0.1 collective-permute-start.6
  24.4 1.6 %collective-permute-start.8 = (f32[176,128]{1,0:T(8,128)S(1)}, f32[176,128]{1,0:T(8,128)S(1)}, u32[]{:S(2)}, u32[]{:S(2)}) collective-permute-start(f32[176,128]{1,0:T(8,128)S(1)} %get-tuple-element.53), channel_id=1, source_target_pairs={{0,6},{1,7},{2,4},{3,5},{4,2},{5,3},{6,0},{7,1},{8,14},{9,15},{10,... | collective-permute-start | bytes 270344 | tf_op jit(solution)/shard_map/ppermute | solution.py:30
  26.0 0.5 %collective-permute-start.7 = (f32[56,128]{1,0:T(8,128)S(1)}, f32[56,128]{1,0:T(8,128)S(1)}, u32[]{:S(2)}, u32[]{:S(2)}) collective-permute-start(f32[56,128]{1,0:T(8,128)S(1)} %get-tuple-element.52), channel_id=1, source_target_pairs={{0,4},{1,5},{2,6},{3,7},{4,0},{5,1},{6,2},{7,3},{8,12},{9,13},{10,... | collective-permute-start | bytes 86024 | tf_op jit(solution)/shard_map/ppermute | solution.py:30
  26.5 2.5 %second.1 = (f32[3,512,128]{2,1,0:T(8,128)S(1)}, f32[512,128]{1,0:T(8,128)S(1)}, f32[512,128]{1,0:T(8,128)S(1)}, f32[7,16,128]{2,1,0:T(8,128)S(1)}) custom-call(f32[9,1184,128]{2,1,0:T(8,128)S(1)} %get-tuple-element.36.ext.refs_0_, f32[3,896,128]{2,1,0:T(8,128)S(1)} %get-tuple-element.38.b0, f32[3,896,128]{2,1,0:T(8,128)S(1)} %get-tuple-element.39.v1, ...), custom_call_target="tpu_custom_call" | custom-call | flops 30000000 | bytes 10000000 | tf_op jit(solution)/shard_map/second/pallas_call | solution.py:641
  29.1 0.9 %collective-permute-done.7.refs_8_ = f32[56,128]{1,0:T(8,128)S(1)} collective-permute-done((f32[56,128]{1,0:T(8,128)S(1)}, f32[56,128]{1,0:T(8,128)S(1)}, u32[]{:S(2)}, u32[]{:S(2)}) %collective-permute-start.7) | collective-permute-done | bytes 28704 | tf_op jit(solution)/shard_map/ppermute | solution.py:30
  30.0 0.0 collective-permute-done.6.refs_7_
  30.0 0.0 collective-permute-done.8.refs_9_
  30.0 3.0 %finish.1 = (f32[3,512,128]{2,1,0:T(8,128)}, f32[512,128]{1,0:T(8,128)}, f32[512,128]{1,0:T(8,128)}) custom-call(f32[9,1184,128]{2,1,0:T(8,128)S(1)} %get-tuple-element.36.ext.refs_0_, f32[9,2,40,128]{3,2,1,0:T(8,128)S(1)} %get-tuple-element.37.refs_1_, f32[3,512,128]{2,1,0:T(8,128)S(1)} %get-tuple-element.43.refs_2_, ...), custom_call_target="tpu_custom_call" | custom-call | tf_op jit(solution)/shard_map/finish/pallas_call | solution.py:652
  (1 shorter events, 0.0 us)
Async XLA Ops:
  2.5 12.5 %collective-permute-start = (f32[616,128]{1,0:T(8,128)S(1)}, f32[616,128]{1,0:T(8,128)S(1)}, u32[]{:S(2)}, u32[]{:S(2)}) collective-permute-start(f32[616,128]{1,0:T(8,128)S(1)} %get-tuple-element.31), channel_id=1, source_target_pairs={{0,8},{1,9},{2,10},{3,11},{4,12},{5,13},{6,14},{7,15},{8,0},{9,1},... | collective-permute-start | bytes 946184 | tf_op jit(solution)/shard_map/ppermute | solution.py:30
  5.6 9.4 %collective-permute-start.1 = (f32[576,128]{1,0:T(8,128)S(1)}, f32[576,128]{1,0:T(8,128)S(1)}, u32[]{:S(2)}, u32[]{:S(2)}) collective-permute-start(f32[576,128]{1,0:T(8,128)S(1)} %get-tuple-element.32), channel_id=1, source_target_pairs={{0,2},{1,3},{2,0},{3,1},{4,6},{5,7},{6,4},{7,5},{8,16},{9,17},{10,... | collective-permute-start | bytes 884744 | tf_op jit(solution)/shard_map/ppermute | solution.py:30
  5.6 9.4 %collective-permute-start.2 = (f32[328,128]{1,0:T(8,128)S(1)}, f32[328,128]{1,0:T(8,128)S(1)}, u32[]{:S(2)}, u32[]{:S(2)}) collective-permute-start(f32[328,128]{1,0:T(8,128)S(1)} %get-tuple-element.33), channel_id=1, source_target_pairs={{0,1},{1,0},{2,3},{3,2},{4,5},{5,4},{6,7},{7,6},{8,9},{9,8},{10,11... | collective-permute-start | bytes 503816 | tf_op jit(solution)/shard_map/ppermute | solution.py:30
  7.1 7.9 %collective-permute-start.3 = (f32[80,128]{1,0:T(8,128)S(1)}, f32[80,128]{1,0:T(8,128)S(1)}, u32[]{:S(2)}, u32[]{:S(2)}) collective-permute-start(f32[80,128]{1,0:T(8,128)S(1)} %get-tuple-element.34), channel_id=1, source_target_pairs={{0,9},{1,8},{2,11},{3,10},{4,13},{5,12},{6,15},{7,14},{8,1},{9,0},... | collective-permute-start | bytes 122888 | tf_op jit(solution)/shard_map/ppermute | solution.py:30
  10.2 3.8 %collective-permute-start.4 = (f32[40,128]{1,0:T(8,128)S(1)}, f32[40,128]{1,0:T(8,128)S(1)}, u32[]{:S(2)}, u32[]{:S(2)}) collective-permute-start(f32[40,128]{1,0:T(8,128)S(1)} %get-tuple-element.35), channel_id=1, source_target_pairs={{0,1},{1,0},{2,3},{3,2},{4,5},{5,4},{6,7},{7,6},{8,17},{9,16},{10,... | collective-permute-start | bytes 61448 | tf_op jit(solution)/shard_map/ppermute | solution.py:30
  15.1 8.1 %collective-permute-start.5 = (f32[160,128]{1,0:T(8,128)S(1)}, f32[160,128]{1,0:T(8,128)S(1)}, u32[]{:S(2)}, u32[]{:S(2)}) collective-permute-start(f32[160,128]{1,0:T(8,128)S(1)} %join.1.refs_0_), channel_id=1, source_target_pairs={{0,16},{1,17},{2,18},{3,19},{4,20},{5,21},{6,22},{7,23},{8,24},{9,... | collective-permute-start | bytes 245768 | tf_op jit(solution)/shard_map/ppermute | solution.py:30
  24.3 5.7 %collective-permute-start.6 = (f32[176,128]{1,0:T(8,128)S(1)}, f32[176,128]{1,0:T(8,128)S(1)}, u32[]{:S(2)}, u32[]{:S(2)}) collective-permute-start(f32[176,128]{1,0:T(8,128)S(1)} %get-tuple-element.51), channel_id=1, source_target_pairs={{0,2},{1,3},{2,0},{3,1},{4,6},{5,7},{6,4},{7,5},{8,10},{9,11},{10,... | collective-permute-start | bytes 270344 | tf_op jit(solution)/shard_map/ppermute | solution.py:30
  24.4 5.6 %collective-permute-start.8 = (f32[176,128]{1,0:T(8,128)S(1)}, f32[176,128]{1,0:T(8,128)S(1)}, u32[]{:S(2)}, u32[]{:S(2)}) collective-permute-start(f32[176,128]{1,0:T(8,128)S(1)} %get-tuple-element.53), channel_id=1, source_target_pairs={{0,6},{1,7},{2,4},{3,5},{4,2},{5,3},{6,0},{7,1},{8,14},{9,15},{10,... | collective-permute-start | bytes 270344 | tf_op jit(solution)/shard_map/ppermute | solution.py:30
  26.0 4.0 %collective-permute-start.7 = (f32[56,128]{1,0:T(8,128)S(1)}, f32[56,128]{1,0:T(8,128)S(1)}, u32[]{:S(2)}, u32[]{:S(2)}) collective-permute-start(f32[56,128]{1,0:T(8,128)S(1)} %get-tuple-element.52), channel_id=1, source_target_pairs={{0,4},{1,5},{2,6},{3,7},{4,0},{5,1},{6,2},{7,3},{8,12},{9,13},{10,... | collective-permute-start | bytes 86024 | tf_op jit(solution)/shard_map/ppermute | solution.py:30
